TPU v7x, 128 devices: a whole 4x4x4 slice. The times are simulated.
128 devices in a mesh: box: 4 (over z_hi, core), samp: 32 (over z_lo, y, x).
Axes of the slice: x: 4, y: 4, z: 4 (z_hi: 2, z_lo: 2; z = z_hi * 2 + z_lo), core: 2. Of those that a mesh axis runs over, the one named last changes fastest.
Arguments:
- child_out: float32 [4096, 2, 18432], P(('box', 'samp')), may hold values from -6 to 6
- child_octant: int32 [512, 8], P(('box', 'samp')), may hold values from 0 to 7, each once within a row
- theta_index: int32 [192, 4], replicated, may hold values from 0 to 95, as said below
- theta_weight: float32 [192, 4], replicated, may hold values from -0.2 to 0.6
- phi_index: int32 [384, 4], replicated, may hold values from 0 to 191, as said below
- phi_weight: float32 [384, 4], replicated, may hold values from -0.2 to 0.6
- shift_angle: float32 [8, 192, 384], replicated, may hold values from -3.140625 to 3.140625
- partner_src: int32 [512, 32], replicated, may hold values from 0 to 511
- partner_disp: int32 [512, 32], replicated, may hold values from 0 to 315
- translation: float32 [316, 2, 192, 384], P(None, None, 'samp'), may hold values from -0.75 to 0.75
Outputs:
- child_in: float32 [4096, 2, 18432], P(('box', 'samp'))
Inputs may be any that keep to these rules, and one draw needn't show every extreme that they name: `theta_index`: four stencil indices for each fine theta sample, consecutive coarse samples near it, clipped to the ends so that they may repeat near the poles (repeated weights add). `phi_index`: four consecutive coarse phi samples near each fine phi sample, wrapping around in phi.
All inputs are finite; a program needn't handle non-finite values.
Results may differ from a plain program's by a relative error of at most 0.00007.
Values sent between devices are 32-bit elements; how exact they have to be, the bound alone decides.
No kernel may reach another device: no remote copies, remote signals or barrier semaphores. Data moves between devices by JAX's collectives and lax.ppermute only.
A program may use at most 256 MiB of HBM per device.

v0:
```python
import jax
import jax.numpy as jnp
from jax import lax
from jax.sharding import PartitionSpec as P

NT1 = 96
NP1 = 192


PRECISE = lax.Precision.HIGHEST


def stencil(index, weight, count):
    hits = (index[:, :, None] == jnp.arange(count, dtype=jnp.int32)[None, None, :]).astype(
        weight.dtype
    )
    return jnp.sum(weight[:, :, None] * hits, axis=1)


def spread(field, theta_mat, phi_mat):
    wider = jnp.einsum("czap,qp->czaq", field, phi_mat, precision=PRECISE)
    return jnp.einsum("ta,czaq->cztq", theta_mat, wider, precision=PRECISE)


def contract(field, theta_mat, phi_mat):
    narrow = jnp.einsum("ta,cztq->czaq", theta_mat, field, precision=PRECISE)
    return jnp.einsum("czaq,qp->czap", narrow, phi_mat, precision=PRECISE)


def rotate(field, cosine, sine_part):
    real_part = field[:, 0]
    imag_part = field[:, 1]
    return jnp.stack(
        [real_part * cosine - imag_part * sine_part, real_part * sine_part + imag_part * cosine],
        axis=1,
    )


def rotate_back(field, cosine, sine_part):
    real_part = field[:, 0]
    imag_part = field[:, 1]
    return jnp.stack(
        [real_part * cosine + imag_part * sine_part, imag_part * cosine - real_part * sine_part],
        axis=1,
    )


def translate_rows(sources, op_table, src_rows, disp_rows):
    receivers = src_rows.shape[0]
    blocks = 4
    per_block = receivers // blocks

    def block_terms(items):
        src_block, disp_block = items
        picked = jnp.take(sources, src_block, axis=0)
        operators = jnp.take(op_table, disp_block, axis=0)
        real_sum = jnp.sum(
            operators[:, :, 0] * picked[:, :, 0] - operators[:, :, 1] * picked[:, :, 1], axis=1
        )
        imag_sum = jnp.sum(
            operators[:, :, 0] * picked[:, :, 1] + operators[:, :, 1] * picked[:, :, 0], axis=1
        )
        return jnp.stack([real_sum, imag_sum], axis=1)

    result = lax.map(
        block_terms,
        (src_rows.reshape(blocks, per_block, -1), disp_rows.reshape(blocks, per_block, -1)),
    )
    return result.reshape((receivers,) + result.shape[2:])


def local(
    child_out,
    child_octant,
    theta_index,
    theta_weight,
    phi_index,
    phi_weight,
    shift_angle,
    partner_src,
    partner_disp,
    translation,
):
    child_count = child_out.shape[0]
    child_grid = child_out.reshape(child_count, 2, NT1, NP1)
    theta_mat = stencil(theta_index, theta_weight, NT1)
    phi_mat = stencil(phi_index, phi_weight, NP1)
    octants = child_octant.reshape(-1)
    onehot = (octants[:, None] == jnp.arange(8, dtype=jnp.int32)[None, :]).astype(jnp.float32)
    cosine = jnp.einsum("co,otq->ctq", onehot, jnp.cos(shift_angle), precision=PRECISE)
    sine_part = jnp.einsum("co,otq->ctq", onehot, jnp.sin(shift_angle), precision=PRECISE)
    fine_child = rotate(spread(child_grid, theta_mat, phi_mat), cosine, sine_part)
    parents = child_octant.shape[0]
    parent_out = jnp.sum(fine_child.reshape((parents, 8) + fine_child.shape[1:]), axis=1)
    box_rank = lax.axis_index("box")
    group_rows = parents * lax.axis_size("samp")
    theta_local = lax.all_to_all(parent_out, "samp", split_axis=2, concat_axis=0, tiled=True)
    all_sources = lax.all_gather(theta_local, "box", axis=0, tiled=True)
    src_rows = lax.dynamic_slice_in_dim(partner_src, box_rank * group_rows, group_rows, 0)
    disp_rows = lax.dynamic_slice_in_dim(partner_disp, box_rank * group_rows, group_rows, 0)
    incoming = translate_rows(all_sources, translation, src_rows, disp_rows)
    parent_in = lax.all_to_all(incoming, "samp", split_axis=0, concat_axis=2, tiled=True)
    repeated = jnp.broadcast_to(parent_in[:, None], (parents, 8) + parent_in.shape[1:]).reshape(
        (parents * 8,) + parent_in.shape[1:]
    )
    result = contract(rotate_back(repeated, cosine, sine_part), theta_mat, phi_mat)
    return result.reshape(child_count, 2, NT1 * NP1)


def solution(mesh):
    in_specs = (
        P(("box", "samp"), None, None),
        P(("box", "samp"), None),
        P(),
        P(),
        P(),
        P(),
        P(),
        P(),
        P(),
        P(None, None, "samp", None),
    )
    out_specs = P(("box", "samp"), None, None)
    return jax.shard_map(local, mesh=mesh, in_specs=in_specs, out_specs=out_specs, check_vma=False)
```

profile of v0, /device:TPU:0, one launch (start us, length us, event | category | flops | bytes accessed | tf_op | source)
XLA Modules:
  0.0 808.1 jit_solution(17452374003100606164)
XLA Ops:
  56.5 25.4 %fusion.6 = f32[32,2,192,384]{3,2,1,0:T(8,128)S(1)} fusion(f32[384,32,2,96]{0,3,2,1:T(8,128)S(1)} %fusion.14, f32[192,96]{1,0:T(8,128)S(1)} %select_reduce_fusion.1), kind=kOutput, calls=%fused_computation.33 | convolution fusion | flops 5435817984 | bytes 28385280 | tf_op jit(solution)/shard_map/ta,czaq->cztq/dot_general | solution.py:22
  81.9 20.8 %multiply_subtract_fusion = (f32[32,192,384]{2,1,0:T(8,128)}, f32[32,192,384]{2,1,0:T(8,128)}) fusion(f32[32,2,192,384]{3,2,1,0:T(8,128)S(1)} %fusion.6, f32[32,192,384]{2,0,1:T(8,128)} %fusion.9, f32[32,192,384]{2,0,1:T(8,128)} %fusion.11), kind=kLoop, calls=%fused_computation.32 | loop fusion | flops 14155776 | bytes 56623104 | tf_op jit(solution)/shard_map/sub | solution.py:34
  112.4 40.3 %all_to_all.33 = f32[4,2,192,384]{3,1,0,2:T(2,128)S(1)} all-to-all(f32[4,2,192,384]{3,1,0,2:T(2,128)S(1)} %copy.114), channel_id=1, replica_groups=mesh['box'=4,'samp'=32] {'samp'}, dimensions={2} | all-to-all | bytes 4718592 | tf_op jit(solution)/shard_map/all_to_all | solution.py:97
  155.9 66.3 %all-gather.2.cloned.1.call-done = f32[512,2,6,384]{3,1,2,0:T(2,128)} async-done(((f32[128,2,6,384]{3,1,2,0:T(2,128)}), f32[512,2,6,384]{3,1,2,0:T(2,128)}) %all-gather.2.cloned.1.call-update) | async-done | bytes 9437200 | tf_op jit(solution)/shard_map/all_gather | solution.py:98
  232.1 438.5 %while.10 = (s32[]{:T(128)}, f32[4,32,2,6,384]{4,2,3,1,0:T(2,128)S(1)}, s32[4,32,32]{2,1,0:T(8,128)S(1)}, f32[316,2,6,384]{3,1,2,0:T(2,128)}, s32[4,32,32]{2,1,0...) while((s32[]{:T(128)}, f32[4,32,2,6,384]{4,2,3,1,0:T(2,128)S(1)}, s32[4,32,32]{2,1,0:T(8,128)S(1)}, ...), condition=%wide.region_6.7_spmd, body=%wide.region_3.6_spmd.sunk | while | flops 28332032 | bytes 191959120 | solution.py:65
  232.2 20.3 %gather_fusion = f32[1024,2,6,384]{3,2,1,0:T(8,128)} fusion(f32[512,2,6,384]{3,2,1,0:T(8,128)} %get-tuple-element.156, s32[1024]{0:T(1024)S(1)} %broadcast_clamp_fusion.4), kind=kCustom, calls=%fused_computation.1.clone.1 | custom fusion | bytes 37752832 | tf_op jit(solution)/shard_map/while/body/eval_jaxpr/jit(_take)/gather | solution.py:55
  270.1 35.1 %gather_fusion.1 = f32[1024,2,6,384]{3,1,2,0:T(2,128)} fusion(f32[316,2,6,384]{3,1,2,0:T(2,128)} %get-tuple-element.154, s32[1024]{0:T(1024)S(1)} %broadcast_clamp_fusion.5), kind=kCustom, calls=%fused_computation.clone.1 | custom fusion | bytes 37752832 | tf_op jit(solution)/shard_map/while/body/eval_jaxpr/jit(_take)/gather | solution.py:56
  305.2 18.1 %copy_select_fusion.2 = f32[32,32,2,6,384]{4,3,2,1,0:T(8,128)} fusion(f32[32,32,2,6,384]{4,2,3,1,0:T(2,128)} %bitcast.113, pred[32,32]{1,0:T(8,128)(4,1)S(1)} %get-tuple-element.134), kind=kLoop, calls=%fused_computation.2.clone.1 | loop fusion | flops 4718592 | bytes 37749760 | tf_op jit(solution)/shard_map/while/body/eval_jaxpr/jit(_take)/select_n | solution.py:56
  323.3 18.0 %subtract_reduce_fusion.2 = (f32[32,6,384]{2,1,0:T(8,128)S(1)}, f32[32,6,384]{2,1,0:T(8,128)S(1)}) fusion(f32[32,32,2,6,384]{4,3,2,1,0:T(8,128)} %broadcast_select_fusion.2, f32[32,32,2,6,384]{4,3,2,1,0:T(8,128)} %copy_select_fusion.2), kind=kLoop, calls=%fused_computation.4.clone.1 | loop fusion | flops 18726912 | bytes 38338560 | tf_op jit(solution)/shard_map/while/body/eval_jaxpr/reduce_sum | solution.py:57
  341.9 20.3 %gather_fusion = f32[1024,2,6,384]{3,2,1,0:T(8,128)} fusion(f32[512,2,6,384]{3,2,1,0:T(8,128)} %get-tuple-element.156, s32[1024]{0:T(1024)S(1)} %broadcast_clamp_fusion.4), kind=kCustom, calls=%fused_computation.1.clone.1 | custom fusion | bytes 37752832 | tf_op jit(solution)/shard_map/while/body/eval_jaxpr/jit(_take)/gather | solution.py:55
  379.7 35.1 %gather_fusion.1 = f32[1024,2,6,384]{3,1,2,0:T(2,128)} fusion(f32[316,2,6,384]{3,1,2,0:T(2,128)} %get-tuple-element.154, s32[1024]{0:T(1024)S(1)} %broadcast_clamp_fusion.5), kind=kCustom, calls=%fused_computation.clone.1 | custom fusion | bytes 37752832 | tf_op jit(solution)/shard_map/while/body/eval_jaxpr/jit(_take)/gather | solution.py:56
  414.8 18.1 %copy_select_fusion.2 = f32[32,32,2,6,384]{4,3,2,1,0:T(8,128)} fusion(f32[32,32,2,6,384]{4,2,3,1,0:T(2,128)} %bitcast.113, pred[32,32]{1,0:T(8,128)(4,1)S(1)} %get-tuple-element.134), kind=kLoop, calls=%fused_computation.2.clone.1 | loop fusion | flops 4718592 | bytes 37749760 | tf_op jit(solution)/shard_map/while/body/eval_jaxpr/jit(_take)/select_n | solution.py:56
  432.9 18.0 %subtract_reduce_fusion.2 = (f32[32,6,384]{2,1,0:T(8,128)S(1)}, f32[32,6,384]{2,1,0:T(8,128)S(1)}) fusion(f32[32,32,2,6,384]{4,3,2,1,0:T(8,128)} %broadcast_select_fusion.2, f32[32,32,2,6,384]{4,3,2,1,0:T(8,128)} %copy_select_fusion.2), kind=kLoop, calls=%fused_computation.4.clone.1 | loop fusion | flops 18726912 | bytes 38338560 | tf_op jit(solution)/shard_map/while/body/eval_jaxpr/reduce_sum | solution.py:57
  451.5 20.3 %gather_fusion = f32[1024,2,6,384]{3,2,1,0:T(8,128)} fusion(f32[512,2,6,384]{3,2,1,0:T(8,128)} %get-tuple-element.156, s32[1024]{0:T(1024)S(1)} %broadcast_clamp_fusion.4), kind=kCustom, calls=%fused_computation.1.clone.1 | custom fusion | bytes 37752832 | tf_op jit(solution)/shard_map/while/body/eval_jaxpr/jit(_take)/gather | solution.py:55
  489.4 35.1 %gather_fusion.1 = f32[1024,2,6,384]{3,1,2,0:T(2,128)} fusion(f32[316,2,6,384]{3,1,2,0:T(2,128)} %get-tuple-element.154, s32[1024]{0:T(1024)S(1)} %broadcast_clamp_fusion.5), kind=kCustom, calls=%fused_computation.clone.1 | custom fusion | bytes 37752832 | tf_op jit(solution)/shard_map/while/body/eval_jaxpr/jit(_take)/gather | solution.py:56
  524.5 18.1 %copy_select_fusion.2 = f32[32,32,2,6,384]{4,3,2,1,0:T(8,128)} fusion(f32[32,32,2,6,384]{4,2,3,1,0:T(2,128)} %bitcast.113, pred[32,32]{1,0:T(8,128)(4,1)S(1)} %get-tuple-element.134), kind=kLoop, calls=%fused_computation.2.clone.1 | loop fusion | flops 4718592 | bytes 37749760 | tf_op jit(solution)/shard_map/while/body/eval_jaxpr/jit(_take)/select_n | solution.py:56
  542.6 18.0 %subtract_reduce_fusion.2 = (f32[32,6,384]{2,1,0:T(8,128)S(1)}, f32[32,6,384]{2,1,0:T(8,128)S(1)}) fusion(f32[32,32,2,6,384]{4,3,2,1,0:T(8,128)} %broadcast_select_fusion.2, f32[32,32,2,6,384]{4,3,2,1,0:T(8,128)} %copy_select_fusion.2), kind=kLoop, calls=%fused_computation.4.clone.1 | loop fusion | flops 18726912 | bytes 38338560 | tf_op jit(solution)/shard_map/while/body/eval_jaxpr/reduce_sum | solution.py:57
  561.2 20.3 %gather_fusion = f32[1024,2,6,384]{3,2,1,0:T(8,128)} fusion(f32[512,2,6,384]{3,2,1,0:T(8,128)} %get-tuple-element.156, s32[1024]{0:T(1024)S(1)} %broadcast_clamp_fusion.4), kind=kCustom, calls=%fused_computation.1.clone.1 | custom fusion | bytes 37752832 | tf_op jit(solution)/shard_map/while/body/eval_jaxpr/jit(_take)/gather | solution.py:55
  599.0 35.1 %gather_fusion.1 = f32[1024,2,6,384]{3,1,2,0:T(2,128)} fusion(f32[316,2,6,384]{3,1,2,0:T(2,128)} %get-tuple-element.154, s32[1024]{0:T(1024)S(1)} %broadcast_clamp_fusion.5), kind=kCustom, calls=%fused_computation.clone.1 | custom fusion | bytes 37752832 | tf_op jit(solution)/shard_map/while/body/eval_jaxpr/jit(_take)/gather | solution.py:56
  634.1 18.1 %copy_select_fusion.2 = f32[32,32,2,6,384]{4,3,2,1,0:T(8,128)} fusion(f32[32,32,2,6,384]{4,2,3,1,0:T(2,128)} %bitcast.113, pred[32,32]{1,0:T(8,128)(4,1)S(1)} %get-tuple-element.134), kind=kLoop, calls=%fused_computation.2.clone.1 | loop fusion | flops 4718592 | bytes 37749760 | tf_op jit(solution)/shard_map/while/body/eval_jaxpr/jit(_take)/select_n | solution.py:56
  652.2 18.0 %subtract_reduce_fusion.2 = (f32[32,6,384]{2,1,0:T(8,128)S(1)}, f32[32,6,384]{2,1,0:T(8,128)S(1)}) fusion(f32[32,32,2,6,384]{4,3,2,1,0:T(8,128)} %broadcast_select_fusion.2, f32[32,32,2,6,384]{4,3,2,1,0:T(8,128)} %copy_select_fusion.2), kind=kLoop, calls=%fused_computation.4.clone.1 | loop fusion | flops 18726912 | bytes 38338560 | tf_op jit(solution)/shard_map/while/body/eval_jaxpr/reduce_sum | solution.py:57
  670.7 39.0 %all_to_all.34 = f32[128,2,6,384]{3,1,2,0:T(2,128)S(1)} all-to-all(f32[128,2,6,384]{3,1,2,0:T(2,128)S(1)} %bitcast.123), channel_id=1, replica_groups=mesh['box'=4,'samp'=32] {'samp'}, dimensions={0} | all-to-all | bytes 4718592 | tf_op jit(solution)/shard_map/all_to_all | solution.py:102
  721.0 21.0 %add_bitcast_fusion = (f32[32,1,192,384]{3,0,2,1:T(8,128)}, f32[32,1,192,384]{3,0,2,1:T(8,128)}) fusion(f32[32,192,384]{2,0,1:T(8,128)} %fusion.9, f32[32,192,384]{2,0,1:T(8,128)} %fusion.11, f32[32,2,192,384]{3,0,2,1:T(8,128)} %broadcast_bitcast_fusion), kind=kLoop, calls=%fused_computation.29 | loop fusion | flops 14155776 | bytes 56623104 | tf_op jit(solution)/shard_map/stack | solution.py:42
  749.1 29.2 %fusion = f32[32,2,384,96]{2,3,1,0:T(8,128)} fusion(f32[32,2,192,384]{3,0,2,1:T(8,128)S(1)} %pad_maximum_fusion, f32[192,96]{1,0:T(8,128)S(1)} %copy-done.3), kind=kOutput, calls=%fused_computation.18 | convolution fusion | flops 5435817984 | bytes 28385280 | tf_op jit(solution)/shard_map/ta,cztq->czaq/dot_general | solution.py:26
  (76 shorter events, 185.7 us)
Async XLA Ops:
  6.5 215.7 %all-gather.2.cloned.1.call-start = ((), (), s32[]{:S(2)}) async-start(), calls=%async_computation.2 | async-start | bytes 11796480 | tf_op jit(solution)/shard_map/all_gather | solution.py:98
  27.4 14.8 %copy-start.4 = (f32[384,4]{0,1:T(4,128)S(1)}, f32[384,4]{0,1:T(4,128)}, u32[]{:S(2)}) copy-start(f32[384,4]{0,1:T(4,128)} %param.17) | copy-start | bytes 18436
  27.4 14.8 %copy-start.5 = (s32[384,4]{0,1:T(4,128)S(1)}, s32[384,4]{0,1:T(4,128)}, u32[]{:S(2)}) copy-start(s32[384,4]{0,1:T(4,128)} %param.16) | copy-start | bytes 18436
  42.4 13.2 %copy-start = (f32[384,192]{0,1:T(8,128)}, f32[384,192]{0,1:T(8,128)S(1)}, u32[]{:S(2)}) copy-start(f32[384,192]{0,1:T(8,128)S(1)} %select_reduce_fusion) | copy-start | bytes 884740
  42.4 13.2 %copy-start.6 = (f32[192,4]{0,1:T(4,128)S(1)}, f32[192,4]{0,1:T(4,128)}, u32[]{:S(2)}) copy-start(f32[192,4]{0,1:T(4,128)} %param.15) | copy-start | bytes 9220
  42.4 13.2 %copy-start.7 = (s32[192,4]{0,1:T(4,128)S(1)}, s32[192,4]{0,1:T(4,128)}, u32[]{:S(2)}) copy-start(s32[192,4]{0,1:T(4,128)} %param.14) | copy-start | bytes 9220
  55.9 0.6 copy-start.2
  742.0 7.1 copy-start.3
  749.1 29.2 %copy-start.1 = (f32[384,192]{0,1:T(8,128)S(1)}, f32[384,192]{0,1:T(8,128)}, u32[]{:S(2)}) copy-start(f32[384,192]{0,1:T(8,128)} %copy-done) | copy-start | bytes 884740
Sparse Core Ops, SparseCore 0:
  155.1 67.1 all-gather.1
where the time goes:
time: 818 us; the launch traced here: 808 us
  local copies, waits for them, and re-layouts  280 us (34%)
  other arithmetic  272 us (33%)
  matrix products  96.5 us (12%)
  blocking collectives  79.3 us (10%)
  waiting for transfers between devices  66.3 us (8%)
  between operations  13.9 us (2%)
    gather x4, local copies, waits for them, and re-layouts, block_terms(): operators = jnp.take(op_table, disp_block, axis=0)  141 us
    gather x4, local copies, waits for them, and re-layouts, block_terms(): picked = jnp.take(sources, src_block, axis=0)  81.3 us
    select_n x4, other arithmetic, block_terms(): operators = jnp.take(op_table, disp_block, axis=0)  72.3 us
    reduce_sum x4, other arithmetic, block_terms(): jnp.sum(operators[:, :, 0] * picked[:, :, 0] - operators[:, :, 1] * picke...  72.1 us
    select_n x8, other arithmetic, block_terms(): picked = jnp.take(sources, src_block, axis=0)  69.7 us
    all_gather x1, waiting for transfers between devices, local(): all_sources = lax.all_gather(theta_local, 'box', axis=0, tiled=True)  66.3 us
    all_to_all x1, blocking collectives, local(): lax.all_to_all(parent_out, 'samp', split_axis=2, concat_axis=0, tiled=True)  40.3 us
    all_to_all x1, blocking collectives, local(): lax.all_to_all(incoming, 'samp', split_axis=0, concat_axis=2, tiled=True)  39 us
  transfers between devices with their start and end apart: 1, of which 1 were waited for; matrix products, arithmetic and copies ran while one was open for 0% of the time, Pallas kernels for 0%

commit v1 on v0

v1 whole, which is shorter than its diff:
```python
import functools

import jax
import jax.numpy as jnp
import numpy as np
from jax import lax
from jax.experimental import pallas as pl
from jax.experimental.pallas import tpu as pltpu
from jax.sharding import Mesh, PartitionSpec as P

NT1, NP1, NT2, NP2 = 96, 192, 192, 384
NDISP, NPART = 316, 32
CHIPS = 64
PARENTS = 4
ROWS = 72
F32, BF16 = jnp.float32, jnp.bfloat16
ALL = ("zh", "c", "zl", "y", "x")
CHIP = ("zh", "zl", "y", "x")


def fit(fn, powers):
    h = 0.7855 * (1 - np.cos(np.pi * (np.arange(400) + 0.5) / 400))
    a = np.stack([h**k for k in powers], 1)
    return [float(v) for v in np.linalg.lstsq(a, fn(h), rcond=None)[0]]


SIN = fit(np.sin, (1, 3, 5, 7, 9, 11))
COS = fit(np.cos, (0, 2, 4, 6, 8, 10))


def horner(z, coefs):
    r = jnp.full_like(z, coefs[-1])
    for c in coefs[-2::-1]:
        r = r * z + c
    return r


def split(x):
    hi = x.astype(BF16)
    return hi, (x - hi.astype(F32)).astype(BF16)


def dot(a, b):
    return jnp.dot(a, b, preferred_element_type=F32)


def stencil_t(index, weight, rows, target):
    n = index.shape[1]
    row = lax.broadcasted_iota(jnp.int32, (rows, n), 0)
    out = jnp.zeros((rows, n), F32)
    for j in range(4):
        out = out + jnp.where(row == target(index[j : j + 1, :]), weight[j : j + 1, :], 0.0)
    return out


def even_odd(a):
    return jnp.where(a % 2 == 0, a // 2, 48 + a // 2)


def unit_row(p, u, part):
    return p * 16 + part * 8 + u if u < 8 else 64 + 2 * p + part


def aggregate_kernel(
    oct_ref, x_ref, angle_ref, ti_ref, tw_ref, pi_ref, pw_ref,
    out_ref, cos_ref, sin_ref,
    t3_ref, pe_ref, po_ref, vh_ref, vl_ref, y3_ref, acc_ref,
):
    p = pl.program_id(0)

    @pl.when(p == 0)
    def _():
        def trig(o, _):
            for r in range(0, NT2, 48):
                h = angle_ref[o, r : r + 48, :] * 0.5
                z = h * h
                s = horner(z, SIN) * h
                c = horner(z, COS)
                cos_ref[o, r : r + 48, :] = 1.0 - 2.0 * (s * s)
                sin_ref[o, r : r + 48, :] = 2.0 * (s * c)
            return 0

        lax.fori_loop(0, 8, trig, 0)
        tt = stencil_t(ti_ref[...], tw_ref[...], 128, even_odd)
        t = jnp.transpose(jnp.concatenate([tt, jnp.zeros((128, 64), F32)], axis=1))[:NT2, :NT1]
        hi, lo = split(t)
        t3_ref[...] = jnp.concatenate([hi, hi, lo], axis=1)
        for ref, shift in ((pe_ref, 0), (po_ref, 64)):
            hi, lo = split(stencil_t(pi_ref[...], pw_ref[...], 256, lambda a: a + shift))
            ref[0], ref[1] = hi, lo

    for k in range(8):
        for part in range(2):
            row = (k * 2 + part) * 48
            for tile in range(3):
                v = x_ref[pl.ds(k * 288 + 2 * tile + part, 48, stride=6), :]
                hi, lo = split(v)
                vh_ref[row : row + 48, tile * 128 : tile * 128 + 128] = hi
                vl_ref[row : row + 48, tile * 128 : tile * 128 + 128] = lo
    for odd, ref in ((0, pe_ref), (1, po_ref)):
        cols = slice(odd * 128, odd * 128 + 256)
        for m in range(0, 768, 192):
            vh, vl = vh_ref[m : m + 192, cols], vl_ref[m : m + 192, cols]
            y = dot(vh, ref[0]) + dot(vl, ref[0]) + dot(vh, ref[1])
            yh, yl = split(y)
            for kk in range(2):
                for part in range(2):
                    r = (kk * 2 + part) * 48
                    for j in range(3):
                        col = j * 256 + part * 128
                        for base, v in ((0, yh), (96, yl), (192, yh)):
                            y3_ref[m // 96 + kk, base + odd * 48 : base + odd * 48 + 48, col : col + 128] = v[
                                r : r + 48, j * 128 : j * 128 + 128
                            ]

    acc_ref[...] = jnp.zeros_like(acc_ref)

    def child(k, _):
        o = oct_ref[p, k]
        for j in range(3):
            f = dot(t3_ref[...], y3_ref[k, :, j * 256 : j * 256 + 256])
            re, im = f[:, :128], f[:, 128:]
            c = cos_ref[o, :, j * 128 : j * 128 + 128]
            s = sin_ref[o, :, j * 128 : j * 128 + 128]
            acc_ref[2 * j] += re * c - im * s
            acc_ref[2 * j + 1] += re * s + im * c
        return 0

    lax.fori_loop(0, 8, child, 0)
    for part in range(2):
        for j in range(3):
            for r in range(3):
                u = r * 3 + j
                base = p * 16 + part * 8 + u if u < 8 else 64 + 2 * p + part
                for zh in range(2):
                    v = acc_ref[2 * j + part, pl.ds(3 * zh + r, 32, stride=6), :]
                    out_ref[pl.ds(zh * 32 * ROWS + base, 32, stride=ROWS), :] = v


def operators_kernel(zh_ref, t_ref, out_ref):
    half = zh_ref[0] * 18

    def one(d, _):
        base = d * 36 + half
        to = pl.multiple_of(d * 24, 8)
        out_ref[pl.ds(to, 8), :] = t_ref[pl.ds(base, 8, stride=2), :]
        out_ref[pl.ds(to + 8, 8), :] = t_ref[pl.ds(base + 1, 8, stride=2), :]
        last = t_ref[pl.ds(base + 16, 2), :]
        out_ref[pl.ds(to + 16, 8), :] = jnp.concatenate([last, last, last, last], axis=0)
        return 0

    lax.fori_loop(0, NDISP, one, 0, unroll=4)


def translate_kernel(src_ref, left_ref, disp_ref, own_ref, other_ref, t_ref, out_ref, s_ref, l_ref, sem):
    n = CHIPS * ROWS
    copies = [
        pltpu.make_async_copy(own_ref, s_ref.at[pl.ds(0, n)], sem.at[0]),
        pltpu.make_async_copy(other_ref, s_ref.at[pl.ds(n, n)], sem.at[1]),
    ]
    for c in copies:
        c.start()
    for c in copies:
        c.wait()

    def spread(i, _):
        v = s_ref[pl.ds(pl.multiple_of(i * ROWS + 64, 8), 8), :]
        for p in range(PARENTS):
            re, im = v[2 * p : 2 * p + 1], v[2 * p + 1 : 2 * p + 2]
            four = jnp.concatenate([re, im, im, re], axis=0)
            l_ref[pl.ds(pl.multiple_of((i * 4 + p) * 8, 8), 8), :] = jnp.concatenate([four, four], axis=0)
        return 0

    lax.fori_loop(0, 2 * CHIPS, spread, 0, unroll=2)

    def receiver(i, _):
        rr = ii = ri = ir = left = None
        for q in range(NPART):
            at = i * NPART + q
            a = pl.multiple_of(src_ref[at], 8)
            b = pl.multiple_of(left_ref[at], 8)
            d = pl.multiple_of(disp_ref[at], 8)
            sr, si = s_ref[pl.ds(a, 8), :], s_ref[pl.ds(a + 8, 8), :]
            tr, ti = t_ref[pl.ds(d, 8), :], t_ref[pl.ds(d + 8, 8), :]
            terms = (tr * sr, ti * si, tr * si, ti * sr, t_ref[pl.ds(d + 16, 8), :] * l_ref[pl.ds(b, 8), :])
            if q == 0:
                rr, ii, ri, ir, left = terms
            else:
                rr, ii, ri, ir, left = rr + terms[0], ii + terms[1], ri + terms[2], ir + terms[3], left + terms[4]
        chip, p = i // PARENTS, i % PARENTS
        base = chip * ROWS
        to = pl.multiple_of(base + p * 16, 8)
        out_ref[pl.ds(to, 8), :] = rr - ii
        out_ref[pl.ds(to + 8, 8), :] = ri + ir
        ends = jnp.concatenate([left[0:1] - left[1:2], left[2:3] + left[3:4]], axis=0)
        out_ref[pl.ds(base + 64 + 2 * p, 2), :] = ends
        return 0

    lax.fori_loop(0, CHIPS * PARENTS, receiver, 0)


def disaggregate_kernel(
    oct_ref, x_ref, cos_ref, sin_ref, ti_ref, tw_ref, pi_ref, pw_ref,
    out_ref,
    t_ref, pe_ref, po_ref, in_ref, r3_ref, z3_ref,
):
    p = pl.program_id(0)

    @pl.when(p == 0)
    def _():
        hi, lo = split(stencil_t(ti_ref[...], tw_ref[...], NT1, even_odd))
        t_ref[...] = jnp.concatenate([hi, hi, lo], axis=1)
        for ref, shift in ((pe_ref, 0), (po_ref, 64)):
            m = jnp.transpose(stencil_t(pi_ref[...], pw_ref[...], 256, lambda a: a + shift))
            hi, lo = split(m)
            ref[...] = jnp.concatenate([hi, hi, lo], axis=0)

    for part in range(2):
        for j in range(3):
            for r in range(3):
                u = r * 3 + j
                base = p * 16 + part * 8 + u if u < 8 else 64 + 2 * p + part
                for zh in range(2):
                    v = x_ref[pl.ds(zh * 32 * ROWS + base, 32, stride=ROWS), :]
                    in_ref[2 * j + part, pl.ds(3 * zh + r, 32, stride=6), :] = v

    def child(k, _):
        o = oct_ref[p, k]
        for j in range(3):
            re, im = in_ref[2 * j], in_ref[2 * j + 1]
            c = cos_ref[o, :, j * 128 : j * 128 + 128]
            s = sin_ref[o, :, j * 128 : j * 128 + 128]
            for part, v in ((0, re * c + im * s), (1, im * c - re * s)):
                hi, lo = split(v)
                cols = slice(part * 128, part * 128 + 128)
                r3_ref[j, 0:192, cols] = hi
                r3_ref[j, 192:384, cols] = lo
                r3_ref[j, 384:576, cols] = hi
            z = dot(t_ref[...], r3_ref[j])
            hi, lo = split(z)
            for part in range(2):
                for odd in range(2):
                    for base, v in ((0, hi), (384, lo), (768, hi)):
                        row = pl.multiple_of((k * 2 + part) * 48, 16)
                        z3_ref[odd, pl.ds(row, 48), base + j * 128 : base + j * 128 + 128] = v[
                            odd * 48 : odd * 48 + 48, part * 128 : part * 128 + 128
                        ]
        return 0

    lax.fori_loop(0, 8, child, 0)
    for k in range(8):
        rows = slice(k * 96, k * 96 + 96)
        even = dot(z3_ref[0, rows, :], pe_ref[...])
        odd = dot(z3_ref[1, rows, :], po_ref[...])
        tiles = (even[:, :128], even[:, 128:] + odd[:, :128], odd[:, 128:])
        for part in range(2):
            for tile in range(3):
                out_ref[pl.ds(k * 288 + 2 * tile + part, 48, stride=6), :] = tiles[tile][part * 48 : part * 48 + 48]


def whole(shape):
    return pl.BlockSpec(shape, lambda *_: (0,) * len(shape))


SMEM = pl.BlockSpec(memory_space=pltpu.SMEM)
LIMIT = 60 * 2**20


def local(
    child_out, child_octant, theta_index, theta_weight, phi_index, phi_weight,
    shift_angle, partner_src, partner_disp, translation,
):
    core = lax.axis_index("c")
    zh = lax.axis_index("zh")
    x = child_out.reshape(32, 2, 144, 128).transpose(0, 2, 1, 3).reshape(32 * 288, 128)
    stencils = (theta_index.T, theta_weight.T, phi_index.T, phi_weight.T)
    stencil_specs = [whole((4, NT2)), whole((4, NT2)), whole((4, NP2)), whole((4, NP2))]
    table = (8, NT2, NP2)
    rows = CHIPS * ROWS
    out, cosine, sine = pl.pallas_call(
        aggregate_kernel,
        grid=(PARENTS,),
        in_specs=[SMEM, pl.BlockSpec((8 * 288, 128), lambda p: (p, 0)), whole(table), *stencil_specs],
        out_specs=[whole((rows, 128)), whole(table), whole(table)],
        out_shape=[
            jax.ShapeDtypeStruct((rows, 128), F32),
            jax.ShapeDtypeStruct(table, F32),
            jax.ShapeDtypeStruct(table, F32),
        ],
        scratch_shapes=[
            pltpu.VMEM((NT2, 288), BF16),
            pltpu.VMEM((2, 256, NP2), BF16),
            pltpu.VMEM((2, 256, NP2), BF16),
            pltpu.VMEM((768, 384), BF16),
            pltpu.VMEM((768, 384), BF16),
            pltpu.VMEM((8, 288, 768), BF16),
            pltpu.VMEM((6, NT2, 128), F32),
        ],
        compiler_params=pltpu.CompilerParams(vmem_limit_bytes=LIMIT),
        cost_estimate=pl.CostEstimate(flops=8 * 10**9, bytes_accessed=14 * 10**6, transcendentals=0),
        name="aggregate",
    )(child_octant, x, shift_angle, *stencils)

    got = lax.all_to_all(out.reshape(CHIPS, ROWS, 128), CHIP, 0, 0, tiled=True).reshape(rows, 128)
    other = lax.ppermute(got, "c", [(0, 1), (1, 0)])

    operators = translation.reshape(NDISP, 2, 6, 3, 128).transpose(0, 2, 3, 1, 4).reshape(NDISP * 36, 128)
    operators = pl.pallas_call(
        operators_kernel,
        in_specs=[SMEM, pl.BlockSpec(memory_space=pltpu.VMEM)],
        out_specs=pl.BlockSpec(memory_space=pltpu.VMEM),
        out_shape=jax.ShapeDtypeStruct((NDISP * 24, 128), F32),
        compiler_params=pltpu.CompilerParams(vmem_limit_bytes=LIMIT),
        cost_estimate=pl.CostEstimate(flops=10**6, bytes_accessed=10**7, transcendentals=0),
        name="operators",
    )(zh.reshape(1), operators)

    def mine(a):
        return lax.dynamic_index_in_dim(a.reshape(2, 2, 128, NPART), core, 1, keepdims=False).reshape(-1)

    src = mine(partner_src)
    holder, p = src // 4, src % 4
    far = jnp.where((holder // 32) % 2 == core, 0, 1)
    chip = far * CHIPS + (holder // 64) * 32 + holder % 32
    src_at = chip * ROWS + p * 16
    left_at = (chip * 4 + p) * 8
    disp_at = mine(partner_disp) * 24
    hbm = pl.BlockSpec(memory_space=pl.ANY)
    incoming = pl.pallas_call(
        translate_kernel,
        in_specs=[SMEM, SMEM, SMEM, hbm, hbm, pl.BlockSpec(memory_space=pltpu.VMEM)],
        out_specs=pl.BlockSpec(memory_space=pltpu.VMEM),
        out_shape=jax.ShapeDtypeStruct((rows, 128), F32),
        scratch_shapes=[
            pltpu.VMEM((2 * rows, 128), F32),
            pltpu.VMEM((512 * 8, 128), F32),
            pltpu.SemaphoreType.DMA((2,)),
        ],
        compiler_params=pltpu.CompilerParams(vmem_limit_bytes=LIMIT),
        cost_estimate=pl.CostEstimate(flops=10**8, bytes_accessed=12 * 10**6, transcendentals=0),
        name="translate",
    )(src_at, left_at, disp_at, got, other, operators)

    back = lax.all_to_all(incoming.reshape(CHIPS, ROWS, 128), CHIP, 0, 0, tiled=True).reshape(rows, 128)
    y = pl.pallas_call(
        disaggregate_kernel,
        grid=(PARENTS,),
        in_specs=[SMEM, whole((rows, 128)), whole(table), whole(table), *stencil_specs],
        out_specs=pl.BlockSpec((8 * 288, 128), lambda p: (p, 0)),
        out_shape=jax.ShapeDtypeStruct((32 * 288, 128), F32),
        scratch_shapes=[
            pltpu.VMEM((NT1, 576), BF16),
            pltpu.VMEM((1152, 256), BF16),
            pltpu.VMEM((1152, 256), BF16),
            pltpu.VMEM((6, NT2, 128), F32),
            pltpu.VMEM((3, 576, 256), BF16),
            pltpu.VMEM((2, 768, 1152), BF16),
        ],
        compiler_params=pltpu.CompilerParams(vmem_limit_bytes=LIMIT),
        cost_estimate=pl.CostEstimate(flops=8 * 10**9, bytes_accessed=14 * 10**6, transcendentals=0),
        name="disaggregate",
    )(child_octant, back, cosine, sine, *stencils)
    return y.reshape(32, 144, 2, 128).transpose(0, 2, 1, 3).reshape(32, 2, NT1 * NP1)


def solution(mesh):
    fine = Mesh(mesh.devices.reshape(2, 2, 2, 4, 4), ALL)
    boxes = P(ALL)
    in_specs = (boxes, boxes, P(), P(), P(), P(), P(), P(), P(), P(None, None, ("zl", "y", "x"), None))
    return jax.shard_map(local, mesh=fine, in_specs=in_specs, out_specs=boxes, check_vma=False)
```

time: 818 us -> 195 us (0.24); the launches traced: 808 us -> 194 us
  other arithmetic: 272 us -> 1.35 us
  local copies, waits for them, and re-layouts: 280 us -> 28 us
  matrix products: 96.5 us -> 0 us
  Pallas kernels: 0 us -> 81 us
  waiting for transfers between devices: 66.3 us -> 0.01 us
  between operations: 13.9 us -> 0.07 us
    gather x8 -> x0, local copies, waits for them, and re-layouts: 222 us -> none  [the longest x4 141 us: block_terms(): operators = jnp.take(op_table, disp_block, axis=0)]
    select_n x12 -> x0, other arithmetic: 142 us -> none  [the longest x4 72.3 us: block_terms(): operators = jnp.take(op_table, disp_block, axis=0)]
    dot_general x6 -> x0, matrix products: 96.5 us -> none  [the longest x1 29.2 us: contract(): narrow = jnp.einsum('ta,cztq->czaq', theta_mat, field, precision=PRECISE)]
    pallas_call x0 -> x4, Pallas kernels: none -> 81 us  [the longest x1 26.3 us: local(): pl.pallas_call(disaggregate_kernel, grid=(PARENTS,), in_specs=[SMEM, whol...]
    reduce_sum x7 -> x0, other arithmetic: 80.3 us -> none  [the longest x4 72.1 us: block_terms(): jnp.sum(operators[:, :, 0] * picked[:, :, 0] - operators[:, :, 1] * picke...]
    all_gather x1 -> x0, waiting for transfers between devices: 66.3 us -> none  [local(): all_sources = lax.all_gather(theta_local, 'box', axis=0, tiled=True)]
    another operation x2 -> x0, other arithmetic: 28.1 us -> none  [rotate_back(): jnp.stack([real_part * cosine + imag_part * sine_part, imag_part * cosine...]
    reshape x3, local copies, waits for them, and re-layouts: 26.1 us -> 0.18 us  [the longest x1 0.09 us: mine(): lax.dynamic_index_in_dim(a.reshape(2, 2, 128, NPART), core, 1, keepdims=F...]
  transfers between devices with their start and end apart: 1 -> 1, of which waited for: 1 -> 0; matrix products, arithmetic and copies ran while one was open for 0% -> 15% of each run, Pallas kernels for 0% -> 3%
where the time goes in v1:
time: 195 us; the launch traced here: 194 us
  blocking collectives  83.9 us (43%)
  Pallas kernels  81 us (42%)
  local copies, waits for them, and re-layouts  28 us (14%)
    all_to_all x1, blocking collectives, local(): lax.all_to_all(out.reshape(CHIPS, ROWS, 128), CHIP, 0, 0, tiled=True)  44.7 us
    all_to_all x1, blocking collectives, local(): lax.all_to_all(incoming.reshape(CHIPS, ROWS, 128), CHIP, 0, 0, tiled=True)  39.2 us
    pallas_call x1, Pallas kernels, local(): pl.pallas_call(disaggregate_kernel, grid=(PARENTS,), in_specs=[SMEM, whol...  26.3 us
    pallas_call x1, Pallas kernels, local(): pl.pallas_call(aggregate_kernel, grid=(PARENTS,), in_specs=[SMEM, pl.Bloc...  25.1 us
    pallas_call x1, Pallas kernels, local(): pl.pallas_call(translate_kernel, in_specs=[SMEM, SMEM, SMEM, hbm, hbm, pl...  24.3 us
    unnamed x9, local copies, waits for them, and re-layouts  13.4 us
    transpose x1, local copies, waits for them, and re-layouts, local(): translation.reshape(NDISP, 2, 6, 3, 128).transpose(0, 2, 3, 1, 4)  13.3 us
    pallas_call x1, Pallas kernels, local(): pl.pallas_call(operators_kernel, in_specs=[SMEM, pl.BlockSpec(memory_spac...  5.3 us
  transfers between devices with their start and end apart: 1, of which 0 were waited for; matrix products, arithmetic and copies ran while one was open for 15% of the time, Pallas kernels for 3%

profile of v1, /device:TPU:0, one launch (start us, length us, event | category | flops | bytes accessed | tf_op | source)
XLA Modules:
  0.0 194.2 jit_solution(4925592953676036304)
XLA Ops:
  0.0 25.1 %aggregate.1 = (f32[4608,128]{1,0:T(8,128)}, f32[8,192,384]{2,1,0:T(8,128)}, f32[8,192,384]{2,1,0:T(8,128)}) custom-call(s32[4,8]{1,0:T(4,128)} %oct_ref.3, f32[9216,128]{1,0:T(8,128)} %bitcast.42, f32[8,192,384]{2,1,0:T(8,128)} %angle_ref.1, s32[4,192]{1,0:T(4,128)} %bitcast.47, f32[4,192]{1,0:T(4,128)} %bitcast.49, s32[4,384]{1,0:T(4,128)} %bitcast.43, ...), custom_call_target="tpu_custom_call" | custom-call | flops 8000000000 | bytes 14000000 | tf_op jit(solution)/shard_map/aggregate/pallas_call | solution.py:280
  25.1 0.0 copy-start.1
  25.1 0.0 copy-start.2
  25.1 44.7 %all_to_all.10 = f32[64,72,128]{2,1,0:T(8,128)S(1)} all-to-all(f32[64,72,128]{2,1,0:T(8,128)} %bitcast.41), channel_id=1, replica_groups=mesh['zh'=2,'c'=2,'zl'=2,'y'=4,'x'=4] {'zh','zl','y','x'}, dimensions={0} | all-to-all | bytes 4718592 | tf_op jit(solution)/shard_map/all_to_all | solution.py:304
  69.8 0.0 copy-start
  69.8 0.0 collective-permute-start
  69.8 0.0 copy-done.1
  69.8 0.0 copy-done.2
  69.9 0.1 constant_dynamic-slice_fusion
  70.0 0.1 copy.21
  70.1 1.0 mul.52.disp_ref
  71.1 0.1 copy.20
  71.2 0.1 reshape.48
  71.3 13.2 %copy.17 = f32[316,2,6,384]{0,3,2,1:T(8,128)} copy(f32[316,2,6,384]{3,1,2,0:T(2,128)} %param.19) | data formatting | bytes 11649024 | tf_op args[9]
  84.5 0.0 copy-done
  84.5 13.3 %copy.18 = f32[316,6,3,2,128]{4,3,2,1,0:T(2,128)} copy(f32[316,6,3,2,128]{0,4,2,1,3:T(8,128)} %bitcast.35) | data formatting | bytes 11649024 | tf_op jit(solution)/shard_map/transpose | solution.py:307
  97.8 5.3 %operators.1.t_ref = f32[7584,128]{1,0:T(8,128)} custom-call(s32[1]{0:T(128)} %bitcast.9.zh_ref, f32[11376,128]{1,0:T(8,128)} %bitcast.36), custom_call_target="tpu_custom_call" | custom-call | flops 1000000 | bytes 10000000 | tf_op jit(solution)/shard_map/operators/pallas_call | solution.py:308
  103.1 0.7 add_multiply_fusion
  103.8 0.6 multiply_add_fusion.src_ref
  104.5 0.0 collective-permute-done.other_ref
  104.5 24.3 %translate.1 = f32[4608,128]{1,0:T(8,128)} custom-call(s32[8192]{0:T(1024)} %multiply_add_fusion.src_ref, s32[8192]{0:T(1024)} %get-tuple-element.11.left_ref, s32[8192]{0:T(1024)} %mul.52.disp_ref, f32[4608,128]{1,0:T(8,128)} %bitcast.38, f32[4608,128]{1,0:T(8,128)} %collective-permute-done.other_ref, f32[7584,128]{1,0:T(8,128)} %operators.1.t_ref), custom_call_target="tpu_custom_call" | custom-call | flops 100000000 | bytes 12000000 | tf_op jit(solution)/shard_map/translate/pallas_call | solution.py:329
  128.8 39.2 %all_to_all.11 = f32[64,72,128]{2,1,0:T(8,128)} all-to-all(f32[64,72,128]{2,1,0:T(8,128)} %bitcast.39), channel_id=1, replica_groups=mesh['zh'=2,'c'=2,'zl'=2,'y'=4,'x'=4] {'zh','zl','y','x'}, dimensions={0} | all-to-all | bytes 4718592 | tf_op jit(solution)/shard_map/all_to_all | solution.py:344
  167.9 26.3 %disaggregate.1 = f32[9216,128]{1,0:T(8,128)} custom-call(s32[4,8]{1,0:T(4,128)} %oct_ref.3, f32[4608,128]{1,0:T(8,128)} %bitcast.40, f32[8,192,384]{2,1,0:T(8,128)} %get-tuple-element.9.cos_ref, f32[8,192,384]{2,1,0:T(8,128)} %get-tuple-element.10.sin_ref, s32[4,192]{1,0:T(4,128)} %bitcast.48, f32[4,192]{1,0:T(4,128)} %bitcast.50, s32[4,384]{1,0:T(4,128)} %bitcast.44, ...), custom_call_target="tpu_custom_call" | custom-call | flops 8000000000 | bytes 14000000 | tf_op jit(solution)/shard_map/disaggregate/pallas_call | solution.py:345
  (3 shorter events, 0.1 us)
Async XLA Ops:
  25.1 44.7 %copy-start.1 = (s32[512,32]{0,1:T(8,128)S(1)}, s32[512,32]{0,1:T(8,128)}, u32[]{:S(2)}) copy-start(s32[512,32]{0,1:T(8,128)} %param.17) | copy-start | bytes 196612
  25.1 44.8 %copy-start.2 = (s32[512,32]{0,1:T(8,128)S(1)}, s32[512,32]{0,1:T(8,128)}, u32[]{:S(2)}) copy-start(s32[512,32]{0,1:T(8,128)} %param.18) | copy-start | bytes 196612
  69.8 14.7 %copy-start = (f32[64,72,128]{2,1,0:T(8,128)}, f32[64,72,128]{2,1,0:T(8,128)S(1)}, u32[]{:S(2)}) copy-start(f32[64,72,128]{2,1,0:T(8,128)S(1)} %all_to_all.10) | copy-start | bytes 7077892
  69.8 34.7 %collective-permute-start = (f32[4608,128]{1,0:T(8,128)S(1)}, f32[4608,128]{1,0:T(8,128)}, u32[]{:S(2)}, u32[]{:S(2)}) collective-permute-start(f32[4608,128]{1,0:T(8,128)S(1)} %bitcast.37), channel_id=1, source_target_pairs={{0,32},{32,0},{1,33},{33,1},{2,34},{34,2},{3,35},{35,3},{4,36},{36... | collective-permute-start | bytes 7077896 | tf_op jit(solution)/shard_map/ppermute | solution.py:305

commit v2 on v1

v2 whole, which is shorter than its diff:
```python
import functools

import jax
import jax.numpy as jnp
import numpy as np
from jax import lax
from jax.experimental import pallas as pl
from jax.experimental.pallas import tpu as pltpu
from jax.sharding import Mesh, PartitionSpec as P

NT1, NP1, NT2, NP2 = 96, 192, 192, 384
NDISP, NPART = 316, 32
CHIPS = 64
PARENTS = 4
FIRST, SECOND = (0, 1), (2,)
F32, BF16 = jnp.float32, jnp.bfloat16
ALL = ("zh", "c", "zl", "y", "x")
CHIP = ("zh", "zl", "y", "x")


def fit(fn, powers):
    h = 0.7855 * (1 - np.cos(np.pi * (np.arange(400) + 0.5) / 400))
    a = np.stack([h**k for k in powers], 1)
    return [float(v) for v in np.linalg.lstsq(a, fn(h), rcond=None)[0]]


SIN = fit(np.sin, (1, 3, 5, 7, 9, 11))
COS = fit(np.cos, (0, 2, 4, 6, 8, 10))


def horner(z, coefs):
    r = jnp.full_like(z, coefs[-1])
    for c in coefs[-2::-1]:
        r = r * z + c
    return r


def split(x):
    hi = x.astype(BF16)
    return hi, (x - hi.astype(F32)).astype(BF16)


def dot(a, b):
    return jnp.dot(a, b, preferred_element_type=F32)


def stencil_t(index, weight, rows, target):
    n = index.shape[1]
    row = lax.broadcasted_iota(jnp.int32, (rows, n), 0)
    out = jnp.zeros((rows, n), F32)
    for j in range(4):
        out = out + jnp.where(row == target(index[j : j + 1, :]), weight[j : j + 1, :], 0.0)
    return out


def even_odd(a):
    return jnp.where(a % 2 == 0, a // 2, 48 + a // 2)


def shape_of(tiles):
    n = len(tiles)
    return n, 3 * n, 6 * n, 24 * n


def aggregate_kernel(tiles, tables, oct_ref, x_ref, angle_ref, ti_ref, tw_ref, pi_ref, pw_ref, out_ref, cos_ref, sin_ref, *scratch):
    t3_ref, pe_ref, po_ref, vh_ref, vl_ref, y3_ref, acc_ref = scratch
    n, half, box, rows = shape_of(tiles)
    p = pl.program_id(0)
    first = tiles[0] if tables else 0
    columns = slice(tiles[0] * 128, tiles[0] * 128 + n * 128)

    @pl.when(p == 0)
    def _():
        def trig(o, _):
            for r in range(0, NT2, 48):
                h = angle_ref[o, r : r + 48, :] * 0.5
                z = h * h
                s = horner(z, SIN) * h
                c = horner(z, COS)
                cos_ref[o, r : r + 48, :] = 1.0 - 2.0 * (s * s)
                sin_ref[o, r : r + 48, :] = 2.0 * (s * c)
            return 0

        lax.fori_loop(0, 8, trig, 0)
        tt = stencil_t(ti_ref[...], tw_ref[...], 128, even_odd)
        t = jnp.transpose(jnp.concatenate([tt, jnp.zeros((128, 64), F32)], axis=1))[:NT2, :NT1]
        hi, lo = split(t)
        t3_ref[...] = jnp.concatenate([hi, hi, lo], axis=1)
        for ref, shift in ((pe_ref, 0), (po_ref, 64)):
            hi, lo = split(stencil_t(pi_ref[:, columns], pw_ref[:, columns], 256, lambda a: a + shift))
            ref[0], ref[1] = hi, lo

    for k in range(8):
        for part in range(2):
            row = (k * 2 + part) * 48
            for tile in range(3):
                v = x_ref[pl.ds(k * 288 + 2 * tile + part, 48, stride=6), :]
                hi, lo = split(v)
                vh_ref[row : row + 48, tile * 128 : tile * 128 + 128] = hi
                vl_ref[row : row + 48, tile * 128 : tile * 128 + 128] = lo
    for odd, ref in ((0, pe_ref), (1, po_ref)):
        cols = slice(odd * 128, odd * 128 + 256)
        for m in range(0, 768, 192):
            vh, vl = vh_ref[m : m + 192, cols], vl_ref[m : m + 192, cols]
            y = dot(vh, ref[0]) + dot(vl, ref[0]) + dot(vh, ref[1])
            yh, yl = split(y)
            for kk in range(2):
                for part in range(2):
                    r = (kk * 2 + part) * 48
                    for j in range(n):
                        col = j * 256 + part * 128
                        for base, v in ((0, yh), (96, yl), (192, yh)):
                            y3_ref[m // 96 + kk, base + odd * 48 : base + odd * 48 + 48, col : col + 128] = v[
                                r : r + 48, j * 128 : j * 128 + 128
                            ]

    for k in range(8):
        o = oct_ref[p, k]
        for j in range(n):
            f = dot(t3_ref[...], y3_ref[k, :, j * 256 : j * 256 + 256])
            re, im = f[:, :128], f[:, 128:]
            at = (first + j) * 128
            c = cos_ref[o, :, at : at + 128]
            s = sin_ref[o, :, at : at + 128]
            if k == 0:
                acc_ref[2 * j] = re * c - im * s
                acc_ref[2 * j + 1] = re * s + im * c
            else:
                acc_ref[2 * j] += re * c - im * s
                acc_ref[2 * j + 1] += re * s + im * c

    for part in range(2):
        for j in range(n):
            for r in range(3):
                base = p * box + part * half + j * 3 + r
                for zh in range(2):
                    v = acc_ref[2 * j + part, pl.ds(3 * zh + r, 32, stride=6), :]
                    out_ref[pl.ds(zh * 32 * rows + base, 32, stride=rows), :] = v


def operators_kernel(zh_ref, t_ref, first_ref, second_ref):
    half = zh_ref[0] * 18

    def one(d, _):
        for ref, tiles, slots in ((first_ref, FIRST, 16), (second_ref, SECOND, 8)):
            gap = 8 if slots == 16 else 3
            for part in range(2):
                for jj, j in enumerate(tiles):
                    v = t_ref[pl.ds(d * 36 + half + j * 2 + part, 3, stride=6), :]
                    ref[pl.ds(d * slots + part * gap + jj * 3, 3), :] = v
        return 0

    lax.fori_loop(0, NDISP, one, 0, unroll=4)


def translate_kernel(tiles, src_ref, disp_ref, own_ref, other_ref, t_ref, out_ref, s_ref):
    n, half, box, rows = shape_of(tiles)
    step = 8 if n == 1 else 16

    def lay(i, _):
        for first, ref in ((0, own_ref), (CHIPS, other_ref)):
            for p in range(PARENTS):
                re = ref[pl.ds(i * rows + p * box, half), :]
                im = ref[pl.ds(i * rows + p * box + half, half), :]
                to = ((first + i) * PARENTS + p) * 16
                s_ref[pl.ds(to, half), :] = re
                s_ref[pl.ds(to + 8, half), :] = im
                if n == 1:
                    s_ref[pl.ds(to + 3, half), :] = im
                    s_ref[pl.ds(to + 11, half), :] = re
        return 0

    lax.fori_loop(0, CHIPS, lay, 0, unroll=2)

    def receiver(i, _):
        sums = None
        for q in range(NPART):
            at = i * NPART + q
            a = pl.multiple_of(src_ref[at] * 16, 8)
            d = pl.multiple_of(disp_ref[at] * step, 8)
            s0, s1 = s_ref[pl.ds(a, 8), :], s_ref[pl.ds(a + 8, 8), :]
            t0 = t_ref[pl.ds(d, 8), :]
            if n == 1:
                terms = (t0 * s0, t0 * s1)
            else:
                t1 = t_ref[pl.ds(d + 8, 8), :]
                terms = (t0 * s0, t1 * s1, t0 * s1, t1 * s0)
            sums = terms if q == 0 else tuple(x + y for x, y in zip(sums, terms))
        if n == 1:
            re, im = sums[0][0:3] - sums[0][3:6], sums[1][0:3] + sums[1][3:6]
        else:
            re, im = (sums[0] - sums[1])[:half], (sums[2] + sums[3])[:half]
        to = (i // PARENTS) * rows + (i % PARENTS) * box
        out_ref[pl.ds(to, half), :] = re
        out_ref[pl.ds(to + half, half), :] = im
        return 0

    lax.fori_loop(0, CHIPS * PARENTS, receiver, 0, unroll=2)


def disaggregate_kernel(tiles, oct_ref, x_ref, cos_ref, sin_ref, ti_ref, tw_ref, pi_ref, pw_ref, *rest):
    (*before_ref, out_ref, t_ref, pe_ref, po_ref, in_ref, r3_ref, z3_ref) = rest
    n, half, box, rows = shape_of(tiles)
    p = pl.program_id(0)
    columns = slice(tiles[0] * 128, tiles[0] * 128 + n * 128)

    @pl.when(p == 0)
    def _():
        hi, lo = split(stencil_t(ti_ref[...], tw_ref[...], NT1, even_odd))
        t_ref[...] = jnp.concatenate([hi, hi, lo], axis=1)
        for ref, shift in ((pe_ref, 0), (po_ref, 64)):
            m = jnp.transpose(stencil_t(pi_ref[:, columns], pw_ref[:, columns], 256, lambda a: a + shift))
            hi, lo = split(m)
            ref[...] = jnp.concatenate([hi, hi, lo], axis=0)

    for part in range(2):
        for j in range(n):
            for r in range(3):
                base = p * box + part * half + j * 3 + r
                for zh in range(2):
                    v = x_ref[pl.ds(zh * 32 * rows + base, 32, stride=rows), :]
                    in_ref[2 * j + part, pl.ds(3 * zh + r, 32, stride=6), :] = v

    for k in range(8):
        o = oct_ref[p, k]
        for j in range(n):
            re, im = in_ref[2 * j], in_ref[2 * j + 1]
            c = cos_ref[o, :, j * 128 : j * 128 + 128]
            s = sin_ref[o, :, j * 128 : j * 128 + 128]
            slot = (k * n + j) % 4
            for part, v in ((0, re * c + im * s), (1, im * c - re * s)):
                hi, lo = split(v)
                cols = slice(part * 128, part * 128 + 128)
                r3_ref[slot, 0:192, cols] = hi
                r3_ref[slot, 192:384, cols] = lo
                r3_ref[slot, 384:576, cols] = hi
            z = dot(t_ref[...], r3_ref[slot])
            hi, lo = split(z)
            for part in range(2):
                for odd in range(2):
                    for base, v in ((0, hi), (n * 128, lo), (n * 256, hi)):
                        row = (k * 2 + part) * 48
                        z3_ref[odd, row : row + 48, base + j * 128 : base + j * 128 + 128] = v[
                            odd * 48 : odd * 48 + 48, part * 128 : part * 128 + 128
                        ]

    for k in range(8):
        span = slice(k * 96, k * 96 + 96)
        even = dot(z3_ref[0, span, :], pe_ref[...])
        odd = dot(z3_ref[1, span, :], po_ref[...])
        blocks = (even[:, :128], even[:, 128:] + odd[:, :128], odd[:, 128:])
        for part in range(2):
            for tile in range(3):
                to = pl.ds(k * 288 + 2 * tile + part, 48, stride=6)
                v = blocks[tile][part * 48 : part * 48 + 48]
                out_ref[to, :] = v + before_ref[0][to, :] if before_ref else v


def whole(shape):
    return pl.BlockSpec(shape, lambda *_: (0,) * len(shape))


VMEM = pl.BlockSpec(memory_space=pltpu.VMEM)
SMEM = pl.BlockSpec(memory_space=pltpu.SMEM)
STENCILS = [whole((4, NT2)), whole((4, NT2)), whole((4, NP2)), whole((4, NP2))]
PARAMS = pltpu.CompilerParams(vmem_limit_bytes=60 * 2**20)
CHILDREN = pl.BlockSpec((8 * 288, 128), lambda p: (p, 0))


def cost(flops, nbytes):
    return pl.CostEstimate(flops=flops, bytes_accessed=nbytes, transcendentals=0)


def table_of(tiles):
    n = len(tiles)
    return pl.BlockSpec((8, NT2, 128 * n), lambda p: (0, 0, tiles[0] // n))


def aggregate(tiles, tables):
    n, _, _, rows = shape_of(tiles)
    table = (8, NT2, NP2)
    part = (8, NT2, 128 * n)
    shapes = [jax.ShapeDtypeStruct((CHIPS * rows, 128), F32)]
    specs = [whole((CHIPS * rows, 128))]
    trig = []
    if tables:
        shapes += [jax.ShapeDtypeStruct(table, F32)] * 2
        specs += [whole(table)] * 2
    else:
        trig = [pltpu.VMEM(part, F32)] * 2
    return pl.pallas_call(
        functools.partial(aggregate_kernel, tiles, tables),
        grid=(PARENTS,),
        in_specs=[SMEM, CHILDREN, whole(table) if tables else table_of(tiles), *STENCILS],
        out_specs=specs,
        out_shape=shapes,
        scratch_shapes=trig
        + [
            pltpu.VMEM((NT2, 288), BF16),
            pltpu.VMEM((2, 256, 128 * n), BF16),
            pltpu.VMEM((2, 256, 128 * n), BF16),
            pltpu.VMEM((768, 384), BF16),
            pltpu.VMEM((768, 384), BF16),
            pltpu.VMEM((8, 288, 256 * n), BF16),
            pltpu.VMEM((2 * n, NT2, 128), F32),
        ],
        compiler_params=PARAMS,
        cost_estimate=cost(n * 4 * 10**9, 10**7),
        name=f"aggregate{n}",
    )


def operators():
    return pl.pallas_call(
        operators_kernel,
        in_specs=[SMEM, VMEM],
        out_specs=[VMEM, VMEM],
        out_shape=[jax.ShapeDtypeStruct((NDISP * 16, 128), F32), jax.ShapeDtypeStruct((NDISP * 8, 128), F32)],
        compiler_params=PARAMS,
        cost_estimate=cost(10**6, 10**7),
        name="operators",
    )


def translate(tiles):
    n, _, _, rows = shape_of(tiles)
    return pl.pallas_call(
        functools.partial(translate_kernel, tiles),
        in_specs=[SMEM, SMEM, VMEM, VMEM, VMEM],
        out_specs=VMEM,
        out_shape=jax.ShapeDtypeStruct((CHIPS * rows, 128), F32),
        scratch_shapes=[pltpu.VMEM((512 * 16, 128), F32)],
        compiler_params=PARAMS,
        cost_estimate=cost(10**8, 10**7),
        name=f"translate{n}",
    )


def disaggregate(tiles, more):
    n, _, _, rows = shape_of(tiles)
    return pl.pallas_call(
        functools.partial(disaggregate_kernel, tiles),
        grid=(PARENTS,),
        in_specs=[SMEM, whole((CHIPS * rows, 128)), table_of(tiles), table_of(tiles), *STENCILS] + [CHILDREN] * more,
        out_specs=CHILDREN,
        out_shape=jax.ShapeDtypeStruct((32 * 288, 128), F32),
        scratch_shapes=[
            pltpu.VMEM((NT1, 576), BF16),
            pltpu.VMEM((384 * n, 256), BF16),
            pltpu.VMEM((384 * n, 256), BF16),
            pltpu.VMEM((2 * n, NT2, 128), F32),
            pltpu.VMEM((4, 576, 256), BF16),
            pltpu.VMEM((2, 768, 384 * n), BF16),
        ],
        compiler_params=PARAMS,
        cost_estimate=cost(n * 4 * 10**9, 10**7),
        name=f"disaggregate{n}",
    )


def exchange(a):
    return lax.all_to_all(a.reshape(CHIPS, -1, 128), CHIP, 0, 0, tiled=True).reshape(a.shape)


def together(*arrays):
    return lax.optimization_barrier(arrays)


def local(
    child_out, child_octant, theta_index, theta_weight, phi_index, phi_weight,
    shift_angle, partner_src, partner_disp, translation,
):
    core = lax.axis_index("c")
    zh = lax.axis_index("zh")
    swap = [(0, 1), (1, 0)]
    x = child_out.reshape(32, 2, 144, 128).transpose(0, 2, 1, 3).reshape(32 * 288, 128)
    stencils = (theta_index.T, theta_weight.T, phi_index.T, phi_weight.T)

    def mine(a):
        return lax.dynamic_index_in_dim(a.reshape(2, 2, 128, NPART), core, 1, keepdims=False).reshape(-1)

    src = mine(partner_src)
    holder, p = src // 4, src % 4
    far = jnp.where((holder // 32) % 2 == core, 0, 1)
    src_at = (far * CHIPS + (holder // 64) * 32 + holder % 32) * PARENTS + p
    disp_at = mine(partner_disp)
    ops, = together(translation.transpose(0, 2, 1, 3).reshape(NDISP * 6, 2, NP2))
    ops = ops.reshape(NDISP * 6, 2, 3, 128).transpose(0, 2, 1, 3).reshape(NDISP * 36, 128)

    (out1,) = aggregate(FIRST, False)(child_octant, x, shift_angle, *stencils)
    got1 = exchange(out1)
    x2, _ = together(x, out1)
    out2, cosine, sine = aggregate(SECOND, True)(child_octant, x2, shift_angle, *stencils)
    ops1, ops2 = operators()(zh.reshape(1), ops)
    got1, out2, ops1, ops2, src_at, disp_at = together(got1, out2, ops1, ops2, src_at, disp_at)

    got2 = exchange(out2)
    other1 = lax.ppermute(got1, "c", swap)
    in1 = translate(FIRST)(src_at, disp_at, got1, other1, ops1)
    in1, got2 = together(in1, got2)

    back1 = exchange(in1)
    other2 = lax.ppermute(got2, "c", swap)
    in2 = translate(SECOND)(src_at, disp_at, got2, other2, ops2)
    in2, back1 = together(in2, back1)

    back2 = exchange(in2)
    y = disaggregate(FIRST, 0)(child_octant, back1, cosine, sine, *stencils)
    y, back2 = together(y, back2)
    y = disaggregate(SECOND, 1)(child_octant, back2, cosine, sine, *stencils, y)
    return y.reshape(32, 144, 2, 128).transpose(0, 2, 1, 3).reshape(32, 2, NT1 * NP1)


def solution(mesh):
    fine = Mesh(mesh.devices.reshape(2, 2, 2, 4, 4), ALL)
    boxes = P(ALL)
    in_specs = (boxes, boxes, P(), P(), P(), P(), P(), P(), P(), P(None, None, ("zl", "y", "x"), None))
    return jax.shard_map(local, mesh=fine, in_specs=in_specs, out_specs=boxes, check_vma=False)
```

time: 195 us -> 153 us (0.78)
  blocking collectives: 83.9 us -> 0 us
  starting transfers between devices: 0.01 us -> 38.1 us
  local copies, waits for them, and re-layouts: 28 us -> 4.07 us
  Pallas kernels: 81 us -> 102 us
  waiting for transfers between devices: 0.01 us -> 7.22 us
    all_to_all x2 -> x0, blocking collectives: 83.9 us -> none  [the longest x1 44.7 us: local(): lax.all_to_all(out.reshape(CHIPS, ROWS, 128), CHIP, 0, 0, tiled=True)]
    all_to_all x0 -> x4, starting transfers between devices: none -> 38 us  [exchange(): lax.all_to_all(a.reshape(CHIPS, -1, 128), CHIP, 0, 0, tiled=True)]
    pallas_call x4 -> x7, Pallas kernels: 81 us -> 102 us  [the longest x1 22.1 us: local(): in1 = translate(FIRST)(src_at, disp_at, got1, other1, ops1)]
    transpose x1 -> x0, local copies, waits for them, and re-layouts: 13.3 us -> none  [local(): translation.reshape(NDISP, 2, 6, 3, 128).transpose(0, 2, 3, 1, 4)]
    unnamed x9 -> x16, local copies, waits for them, and re-layouts: 13.4 us -> 3.11 us
    all_to_all x0 -> x4, waiting for transfers between devices: none -> 4.94 us  [exchange(): lax.all_to_all(a.reshape(CHIPS, -1, 128), CHIP, 0, 0, tiled=True)]
    ppermute x1 -> x2, waiting for transfers between devices: 0.01 us -> 2.27 us  [the longest x1 2.27 us: local(): other2 = lax.ppermute(got2, 'c', swap)]
  transfers between devices with their start and end apart: 1 -> 6, of which waited for: 0 -> 3; matrix products, arithmetic and copies ran while one was open for 15% -> 1% of each run, Pallas kernels for 3% -> 52%
where the time goes in v2:
time: 153 us; the launch traced here: 152 us
  Pallas kernels  102 us (67%)
  starting transfers between devices  38.1 us (25%)
  waiting for transfers between devices  7.22 us (5%)
  local copies, waits for them, and re-layouts  4.07 us (3%)
    all_to_all x4, starting transfers between devices, exchange(): lax.all_to_all(a.reshape(CHIPS, -1, 128), CHIP, 0, 0, tiled=True)  38 us
    pallas_call x1, Pallas kernels, local(): in1 = translate(FIRST)(src_at, disp_at, got1, other1, ops1)  22.1 us
    pallas_call x1, Pallas kernels, local(): in2 = translate(SECOND)(src_at, disp_at, got2, other2, ops2)  21.1 us
    pallas_call x1, Pallas kernels, local(): y = disaggregate(FIRST, 0)(child_octant, back1, cosine, sine, *stencils)  17.6 us
    pallas_call x1, Pallas kernels, local(): out1, = aggregate(FIRST, False)(child_octant, x, shift_angle, *stencils)  12.6 us
    pallas_call x1, Pallas kernels, local(): aggregate(SECOND, True)(child_octant, x2, shift_angle, *stencils)  11.9 us
    pallas_call x1, Pallas kernels, local(): y = disaggregate(SECOND, 1)(child_octant, back2, cosine, sine, *stencils, y)  10.4 us
    pallas_call x1, Pallas kernels, local(): ops1, ops2 = operators()(zh.reshape(1), ops)  5.8 us
  transfers between devices with their start and end apart: 6, of which 3 were waited for; matrix products, arithmetic and copies ran while one was open for 1% of the time, Pallas kernels for 52%

profile of v2, /device:TPU:0, one launch (start us, length us, event | category | flops | bytes accessed | tf_op | source)
XLA Modules:
  0.0 151.8 jit_solution(6427419259256499341)
XLA Ops:
  0.0 12.6 %aggregate2.1 = f32[3072,128]{1,0:T(8,128)} custom-call(s32[4,8]{1,0:T(4,128)} %oct_ref.7, f32[9216,128]{1,0:T(8,128)} %bitcast.70, f32[8,192,384]{2,1,0:T(8,128)} %angle_ref.3, s32[4,192]{1,0:T(4,128)} %bitcast.62, f32[4,192]{1,0:T(4,128)} %bitcast.66, s32[4,384]{1,0:T(4,128)} %bitcast.54, f32[4,384]{1,0:T(4,128)} %bitcast.58), custom_call_target="tpu_custom_call" | custom-call | flops 8000000000 | bytes 10000000 | tf_op jit(solution)/shard_map/aggregate2/pallas_call | solution.py:390
  12.6 11.7 %all-to-all-start = ((f32[64,48,128]{2,1,0:T(8,128)}), f32[64,48,128]{2,1,0:T(8,128)S(1)}, u32[]{:S(2)}, u32[]{:S(2)}) async-start(f32[64,48,128]{2,1,0:T(8,128)} %bitcast.51), calls=%async_computation | async-start | bytes 3145728 | tf_op jit(solution)/shard_map/all_to_all | solution.py:362
  24.4 0.1 constant_dynamic-slice_fusion
  24.5 0.1 copy.18
  24.6 0.7 reshape.73.disp_ref
  25.3 0.1 copy.17
  25.4 0.1 reshape.71
  25.5 5.8 %operators.1 = (f32[5056,128]{1,0:T(8,128)}, f32[2528,128]{1,0:T(8,128)}) custom-call(s32[1]{0:T(128)} %bitcast.11.zh_ref, f32[11376,128]{1,0:T(8,128)} %bitcast.46), custom_call_target="tpu_custom_call" | custom-call | flops 1000000 | bytes 10000000 | tf_op jit(solution)/shard_map/operators/pallas_call | solution.py:394
  31.3 0.7 fusion.7.src_ref
  32.0 11.9 %aggregate1.1 = (f32[1536,128]{1,0:T(8,128)}, f32[8,192,384]{2,1,0:T(8,128)}, f32[8,192,384]{2,1,0:T(8,128)}) custom-call(s32[4,8]{1,0:T(4,128)} %oct_ref.7, f32[9216,128]{1,0:T(8,128)} %bitcast.71, f32[8,192,384]{2,1,0:T(8,128)} %angle_ref.3, s32[4,192]{1,0:T(4,128)} %bitcast.63, f32[4,192]{1,0:T(4,128)} %bitcast.67, s32[4,384]{1,0:T(4,128)} %bitcast.55, ...), custom_call_target="tpu_custom_call" | custom-call | flops 4000000000 | bytes 10000000 | tf_op jit(solution)/shard_map/aggregate1/pallas_call | solution.py:393
  44.0 4.8 %all-to-all-done = f32[64,48,128]{2,1,0:T(8,128)S(1)} async-done(((f32[64,48,128]{2,1,0:T(8,128)}), f32[64,48,128]{2,1,0:T(8,128)S(1)}, u32[]{:S(2)}, u32[]{:S(2)}) %all-to-all-start) | async-done | bytes 1572896 | tf_op jit(solution)/shard_map/all_to_all | solution.py:362
  48.7 5.7 %all-to-all-start.1 = ((f32[64,24,128]{2,1,0:T(8,128)}), f32[64,24,128]{2,1,0:T(8,128)S(1)}, u32[]{:S(2)}, u32[]{:S(2)}) async-start(f32[64,24,128]{2,1,0:T(8,128)} %bitcast.53), calls=%async_computation.1 | async-start | bytes 1572864 | tf_op jit(solution)/shard_map/all_to_all | solution.py:362
  54.5 22.1 %translate2.1 = f32[3072,128]{1,0:T(8,128)} custom-call(s32[8192]{0:T(1024)} %fusion.7.src_ref, s32[8192]{0:T(1024)} %reshape.73.disp_ref, f32[3072,128]{1,0:T(8,128)} %bitcast.44, f32[3072,128]{1,0:T(8,128)} %collective-permute-done.other_ref, f32[5056,128]{1,0:T(8,128)} %get-tuple-element.30.t_ref), custom_call_target="tpu_custom_call" | custom-call | flops 100000000 | bytes 10000000 | tf_op jit(solution)/shard_map/translate2/pallas_call | solution.py:399
  76.6 10.3 %all-to-all-start.2 = ((f32[64,48,128]{2,1,0:T(8,128)}), f32[64,48,128]{2,1,0:T(8,128)S(1)}, u32[]{:S(2)}, u32[]{:S(2)}) async-start(f32[64,48,128]{2,1,0:T(8,128)} %bitcast.45), calls=%async_computation.2 | async-start | bytes 3145728 | tf_op jit(solution)/shard_map/all_to_all | solution.py:362
  86.9 0.1 collective-permute-start.1
  87.0 2.3 %collective-permute-done.1.other_ref = f32[1536,128]{1,0:T(8,128)S(1)} collective-permute-done((f32[1536,128]{1,0:T(8,128)S(1)}, f32[1536,128]{1,0:T(8,128)S(1)}, u32[]{:S(2)}, u32[]{:S(2)}) %collective-permute-start.1) | collective-permute-done | bytes 786464 | tf_op jit(solution)/shard_map/ppermute | solution.py:403
  89.3 0.9 copy-done.4
  90.2 21.1 %translate1.1 = f32[1536,128]{1,0:T(8,128)} custom-call(s32[8192]{0:T(1024)} %fusion.7.src_ref, s32[8192]{0:T(1024)} %reshape.73.disp_ref, f32[1536,128]{1,0:T(8,128)} %bitcast.48, f32[1536,128]{1,0:T(8,128)} %copy-done.4, f32[2528,128]{1,0:T(8,128)} %get-tuple-element.33.t_ref), custom_call_target="tpu_custom_call" | custom-call | flops 100000000 | bytes 10000000 | tf_op jit(solution)/shard_map/translate1/pallas_call | solution.py:404
  111.2 0.2 all-to-all-done.2
  111.4 1.1 copy-done.3
  112.6 10.3 %all-to-all-start.3 = ((f32[64,24,128]{2,1,0:T(8,128)}), f32[64,24,128]{2,1,0:T(8,128)S(1)}, u32[]{:S(2)}, u32[]{:S(2)}) async-start(f32[64,24,128]{2,1,0:T(8,128)} %bitcast.49), calls=%async_computation.3 | async-start | bytes 1572864 | tf_op jit(solution)/shard_map/all_to_all | solution.py:362
  122.9 17.6 %disaggregate2.1.rest_0_ = f32[9216,128]{1,0:T(8,128)} custom-call(s32[4,8]{1,0:T(4,128)} %oct_ref.7, f32[3072,128]{1,0:T(8,128)} %bitcast.52, f32[8,192,384]{2,1,0:T(8,128)} %get-tuple-element.36.cos_ref, f32[8,192,384]{2,1,0:T(8,128)} %get-tuple-element.37.sin_ref, s32[4,192]{1,0:T(4,128)} %bitcast.64, f32[4,192]{1,0:T(4,128)} %bitcast.68, ...), custom_call_target="tpu_custom_call" | custom-call | flops 8000000000 | bytes 10000000 | tf_op jit(solution)/shard_map/disaggregate2/pallas_call | solution.py:408
  140.5 0.9 copy-done.2
  141.4 10.4 %disaggregate1.1 = f32[9216,128]{1,0:T(8,128)} custom-call(s32[4,8]{1,0:T(4,128)} %oct_ref.7, f32[1536,128]{1,0:T(8,128)} %bitcast.50, f32[8,192,384]{2,1,0:T(8,128)} %get-tuple-element.36.cos_ref, f32[8,192,384]{2,1,0:T(8,128)} %get-tuple-element.37.sin_ref, s32[4,192]{1,0:T(4,128)} %bitcast.65, f32[4,192]{1,0:T(4,128)} %bitcast.69, s32[4,384]{1,0:T(4,128)} %bitcast.57, ...), custom_call_target="tpu_custom_call" | custom-call | flops 4000000000 | bytes 10000000 | tf_op jit(solution)/shard_map/disaggregate1/pallas_call | solution.py:410
  (17 shorter events, 0.1 us)
Async XLA Ops:
  12.6 11.7 %copy-start.5 = (s32[512,32]{0,1:T(8,128)S(1)}, s32[512,32]{0,1:T(8,128)}, u32[]{:S(2)}) copy-start(s32[512,32]{0,1:T(8,128)} %param.17) | copy-start | bytes 196612
  12.6 11.7 %copy-start.6 = (s32[512,32]{0,1:T(8,128)S(1)}, s32[512,32]{0,1:T(8,128)}, u32[]{:S(2)}) copy-start(s32[512,32]{0,1:T(8,128)} %param.18) | copy-start | bytes 196612
  12.6 36.1 %all-to-all-start = ((f32[64,48,128]{2,1,0:T(8,128)}), f32[64,48,128]{2,1,0:T(8,128)S(1)}, u32[]{:S(2)}, u32[]{:S(2)}) async-start(f32[64,48,128]{2,1,0:T(8,128)} %bitcast.51), calls=%async_computation | async-start | bytes 3145728 | tf_op jit(solution)/shard_map/all_to_all | solution.py:362
  48.7 5.7 %copy-start = (f32[64,48,128]{2,1,0:T(8,128)}, f32[64,48,128]{2,1,0:T(8,128)S(1)}, u32[]{:S(2)}) copy-start(f32[64,48,128]{2,1,0:T(8,128)S(1)} %all-to-all-done) | copy-start | bytes 4718596
  48.7 5.7 %collective-permute-start = (f32[3072,128]{1,0:T(8,128)S(1)}, f32[3072,128]{1,0:T(8,128)}, u32[]{:S(2)}, u32[]{:S(2)}) collective-permute-start(f32[3072,128]{1,0:T(8,128)S(1)} %bitcast.43), channel_id=1, source_target_pairs={{0,32},{32,0},{1,33},{33,1},{2,34},{34,2},{3,35},{35,3},{4,36},{36... | collective-permute-start | bytes 4718600 | tf_op jit(solution)/shard_map/ppermute | solution.py:398
  48.7 27.8 %all-to-all-start.1 = ((f32[64,24,128]{2,1,0:T(8,128)}), f32[64,24,128]{2,1,0:T(8,128)S(1)}, u32[]{:S(2)}, u32[]{:S(2)}) async-start(f32[64,24,128]{2,1,0:T(8,128)} %bitcast.53), calls=%async_computation.1 | async-start | bytes 1572864 | tf_op jit(solution)/shard_map/all_to_all | solution.py:362
  76.6 12.7 %copy-start.1 = (f32[64,24,128]{2,1,0:T(8,128)}, f32[64,24,128]{2,1,0:T(8,128)S(1)}, u32[]{:S(2)}) copy-start(f32[64,24,128]{2,1,0:T(8,128)S(1)} %all-to-all-done.1) | copy-start | bytes 2359300
  76.6 34.9 %all-to-all-start.2 = ((f32[64,48,128]{2,1,0:T(8,128)}), f32[64,48,128]{2,1,0:T(8,128)S(1)}, u32[]{:S(2)}, u32[]{:S(2)}) async-start(f32[64,48,128]{2,1,0:T(8,128)} %bitcast.45), calls=%async_computation.2 | async-start | bytes 3145728 | tf_op jit(solution)/shard_map/all_to_all | solution.py:362
  86.9 2.4 %collective-permute-start.1 = (f32[1536,128]{1,0:T(8,128)S(1)}, f32[1536,128]{1,0:T(8,128)S(1)}, u32[]{:S(2)}, u32[]{:S(2)}) collective-permute-start(f32[1536,128]{1,0:T(8,128)S(1)} %bitcast.47), channel_id=1, source_target_pairs={{0,32},{32,0},{1,33},{33,1},{2,34},{34,2},{3,35},{35,3},{4,36},{36... | collective-permute-start | bytes 2359304 | tf_op jit(solution)/shard_map/ppermute | solution.py:403
  89.3 0.9 copy-start.4
  111.4 1.1 copy-start.3
  112.6 27.9 %all-to-all-start.3 = ((f32[64,24,128]{2,1,0:T(8,128)}), f32[64,24,128]{2,1,0:T(8,128)S(1)}, u32[]{:S(2)}, u32[]{:S(2)}) async-start(f32[64,24,128]{2,1,0:T(8,128)} %bitcast.49), calls=%async_computation.3 | async-start | bytes 1572864 | tf_op jit(solution)/shard_map/all_to_all | solution.py:362
  140.5 0.9 copy-start.2

commit v3 on v2

--- a/solution.py
+++ b/solution.py
@@ -12,6 +12,7 @@
 NDISP, NPART = 316, 32
 CHIPS = 64
 PARENTS = 4
+SLOT = 16
 FIRST, SECOND = (0, 1), (2,)
 F32, BF16 = jnp.float32, jnp.bfloat16
 ALL = ("zh", "c", "zl", "y", "x")
@@ -142,12 +143,12 @@
     half = zh_ref[0] * 18
 
     def one(d, _):
-        for ref, tiles, slots in ((first_ref, FIRST, 16), (second_ref, SECOND, 8)):
-            gap = 8 if slots == 16 else 3
+        for ref, tiles in ((first_ref, FIRST), (second_ref, SECOND)):
+            gap = 8 if len(tiles) == 2 else 3
             for part in range(2):
                 for jj, j in enumerate(tiles):
                     v = t_ref[pl.ds(d * 36 + half + j * 2 + part, 3, stride=6), :]
-                    ref[pl.ds(d * slots + part * gap + jj * 3, 3), :] = v
+                    ref[pl.ds(d * SLOT + part * gap + jj * 3, 3), :] = v
         return 0
 
     lax.fori_loop(0, NDISP, one, 0, unroll=4)
@@ -155,7 +156,6 @@
 
 def translate_kernel(tiles, src_ref, disp_ref, own_ref, other_ref, t_ref, out_ref, s_ref):
     n, half, box, rows = shape_of(tiles)
-    step = 8 if n == 1 else 16
 
     def lay(i, _):
         for first, ref in ((0, own_ref), (CHIPS, other_ref)):
@@ -176,8 +176,8 @@
         sums = None
         for q in range(NPART):
             at = i * NPART + q
-            a = pl.multiple_of(src_ref[at] * 16, 8)
-            d = pl.multiple_of(disp_ref[at] * step, 8)
+            a = pl.multiple_of(src_ref[at], 8)
+            d = pl.multiple_of(disp_ref[at], 8)
             s0, s1 = s_ref[pl.ds(a, 8), :], s_ref[pl.ds(a + 8, 8), :]
             t0 = t_ref[pl.ds(d, 8), :]
             if n == 1:
@@ -199,15 +199,14 @@
 
 
 def disaggregate_kernel(tiles, oct_ref, x_ref, cos_ref, sin_ref, ti_ref, tw_ref, pi_ref, pw_ref, *rest):
-    (*before_ref, out_ref, t_ref, pe_ref, po_ref, in_ref, r3_ref, z3_ref) = rest
+    (*before_ref, out_ref, t_ref, pe_ref, po_ref, in_ref, z3_ref) = rest
     n, half, box, rows = shape_of(tiles)
     p = pl.program_id(0)
     columns = slice(tiles[0] * 128, tiles[0] * 128 + n * 128)
 
     @pl.when(p == 0)
     def _():
-        hi, lo = split(stencil_t(ti_ref[...], tw_ref[...], NT1, even_odd))
-        t_ref[...] = jnp.concatenate([hi, hi, lo], axis=1)
+        t_ref[...] = jnp.concatenate(split(stencil_t(ti_ref[...], tw_ref[...], NT1, even_odd)), axis=0)
         for ref, shift in ((pe_ref, 0), (po_ref, 64)):
             m = jnp.transpose(stencil_t(pi_ref[:, columns], pw_ref[:, columns], 256, lambda a: a + shift))
             hi, lo = split(m)
@@ -227,14 +226,9 @@
             re, im = in_ref[2 * j], in_ref[2 * j + 1]
             c = cos_ref[o, :, j * 128 : j * 128 + 128]
             s = sin_ref[o, :, j * 128 : j * 128 + 128]
-            slot = (k * n + j) % 4
-            for part, v in ((0, re * c + im * s), (1, im * c - re * s)):
-                hi, lo = split(v)
-                cols = slice(part * 128, part * 128 + 128)
-                r3_ref[slot, 0:192, cols] = hi
-                r3_ref[slot, 192:384, cols] = lo
-                r3_ref[slot, 384:576, cols] = hi
-            z = dot(t_ref[...], r3_ref[slot])
+            hi, lo = split(jnp.concatenate([re * c + im * s, im * c - re * s], axis=1))
+            g = dot(t_ref[...], hi)
+            z = g[:NT1] + g[NT1:] + dot(t_ref[:NT1], lo)
             hi, lo = split(z)
             for part in range(2):
                 for odd in range(2):
@@ -244,16 +238,18 @@
                             odd * 48 : odd * 48 + 48, part * 128 : part * 128 + 128
                         ]
 
-    for k in range(8):
-        span = slice(k * 96, k * 96 + 96)
+    for first in range(0, 8, 4):
+        span = slice(first * 96, first * 96 + 384)
         even = dot(z3_ref[0, span, :], pe_ref[...])
         odd = dot(z3_ref[1, span, :], po_ref[...])
         blocks = (even[:, :128], even[:, 128:] + odd[:, :128], odd[:, 128:])
-        for part in range(2):
-            for tile in range(3):
-                to = pl.ds(k * 288 + 2 * tile + part, 48, stride=6)
-                v = blocks[tile][part * 48 : part * 48 + 48]
-                out_ref[to, :] = v + before_ref[0][to, :] if before_ref else v
+        for k in range(4):
+            for part in range(2):
+                at = (k * 2 + part) * 48
+                for tile in range(3):
+                    to = pl.ds((first + k) * 288 + 2 * tile + part, 48, stride=6)
+                    v = blocks[tile][at : at + 48]
+                    out_ref[to, :] = v + before_ref[0][to, :] if before_ref else v
 
 
 def whole(shape):
@@ -315,7 +311,7 @@
         operators_kernel,
         in_specs=[SMEM, VMEM],
         out_specs=[VMEM, VMEM],
-        out_shape=[jax.ShapeDtypeStruct((NDISP * 16, 128), F32), jax.ShapeDtypeStruct((NDISP * 8, 128), F32)],
+        out_shape=[jax.ShapeDtypeStruct((NDISP * SLOT, 128), F32)] * 2,
         compiler_params=PARAMS,
         cost_estimate=cost(10**6, 10**7),
         name="operators",
@@ -345,11 +341,10 @@
         out_specs=CHILDREN,
         out_shape=jax.ShapeDtypeStruct((32 * 288, 128), F32),
         scratch_shapes=[
-            pltpu.VMEM((NT1, 576), BF16),
+            pltpu.VMEM((2 * NT1, NT2), BF16),
             pltpu.VMEM((384 * n, 256), BF16),
             pltpu.VMEM((384 * n, 256), BF16),
             pltpu.VMEM((2 * n, NT2, 128), F32),
-            pltpu.VMEM((4, 576, 256), BF16),
             pltpu.VMEM((2, 768, 384 * n), BF16),
         ],
         compiler_params=PARAMS,
@@ -382,8 +377,8 @@
     src = mine(partner_src)
     holder, p = src // 4, src % 4
     far = jnp.where((holder // 32) % 2 == core, 0, 1)
-    src_at = (far * CHIPS + (holder // 64) * 32 + holder % 32) * PARENTS + p
-    disp_at = mine(partner_disp)
+    src_at = ((far * CHIPS + (holder // 64) * 32 + holder % 32) * PARENTS + p) * SLOT
+    disp_at = mine(partner_disp) * SLOT
     ops, = together(translation.transpose(0, 2, 1, 3).reshape(NDISP * 6, 2, NP2))
     ops = ops.reshape(NDISP * 6, 2, 3, 128).transpose(0, 2, 1, 3).reshape(NDISP * 36, 128)
 

time: 153 us -> 140 us (0.915)
  Pallas kernels: 102 us -> 84.7 us
  waiting for transfers between devices: 7.22 us -> 15.9 us
  starting transfers between devices: 38.1 us -> 34.1 us
    all_to_all x4, waiting for transfers between devices: 4.94 us -> 13.6 us  [exchange(): lax.all_to_all(a.reshape(CHIPS, -1, 128), CHIP, 0, 0, tiled=True)]
    pallas_call x1, Pallas kernels: 17.6 us -> 11.6 us  [local(): y = disaggregate(FIRST, 0)(child_octant, back1, cosine, sine, *stencils)]
    pallas_call x1, Pallas kernels: 22.1 us -> 17.4 us  [local(): in1 = translate(FIRST)(src_at, disp_at, got1, other1, ops1)]
    pallas_call x1, Pallas kernels: 21.1 us -> 16.8 us  [local(): in2 = translate(SECOND)(src_at, disp_at, got2, other2, ops2)]
    all_to_all x4, starting transfers between devices: 38 us -> 34 us  [exchange(): lax.all_to_all(a.reshape(CHIPS, -1, 128), CHIP, 0, 0, tiled=True)]
    pallas_call x1, Pallas kernels: 10.4 us -> 8.31 us  [local(): y = disaggregate(SECOND, 1)(child_octant, back2, cosine, sine, *stencils, y)]
  transfers between devices with their start and end apart: 6 -> 6, of which waited for: 3 -> 4; matrix products, arithmetic and copies ran while one was open for 1% -> 1% of each run, Pallas kernels for 52% -> 46%
where the time goes in v3:
time: 140 us
  Pallas kernels  84.7 us (60%)
  starting transfers between devices  34.1 us (24%)
  waiting for transfers between devices  15.9 us (11%)
  local copies, waits for them, and re-layouts  4.05 us (3%)
    all_to_all x4, starting transfers between devices, exchange(): lax.all_to_all(a.reshape(CHIPS, -1, 128), CHIP, 0, 0, tiled=True)  34 us
    pallas_call x1, Pallas kernels, local(): in1 = translate(FIRST)(src_at, disp_at, got1, other1, ops1)  17.4 us
    pallas_call x1, Pallas kernels, local(): in2 = translate(SECOND)(src_at, disp_at, got2, other2, ops2)  16.8 us
    all_to_all x4, waiting for transfers between devices, exchange(): lax.all_to_all(a.reshape(CHIPS, -1, 128), CHIP, 0, 0, tiled=True)  13.6 us
    pallas_call x1, Pallas kernels, local(): out1, = aggregate(FIRST, False)(child_octant, x, shift_angle, *stencils)  12.6 us
    pallas_call x1, Pallas kernels, local(): aggregate(SECOND, True)(child_octant, x2, shift_angle, *stencils)  11.9 us
    pallas_call x1, Pallas kernels, local(): y = disaggregate(FIRST, 0)(child_octant, back1, cosine, sine, *stencils)  11.6 us
    pallas_call x1, Pallas kernels, local(): y = disaggregate(SECOND, 1)(child_octant, back2, cosine, sine, *stencils, y)  8.31 us
  transfers between devices with their start and end apart: 6, of which 4 were waited for; matrix products, arithmetic and copies ran while one was open for 1% of the time, Pallas kernels for 46%

profile of v3, /device:TPU:0, one launch (start us, length us, event | category | flops | bytes accessed | tf_op | source)
XLA Modules:
  0.0 139.6 jit_solution(6121772454631287188)
XLA Ops:
  0.0 12.6 %aggregate2.1 = f32[3072,128]{1,0:T(8,128)} custom-call(s32[4,8]{1,0:T(4,128)} %oct_ref.7, f32[9216,128]{1,0:T(8,128)} %bitcast.70, f32[8,192,384]{2,1,0:T(8,128)} %angle_ref.3, s32[4,192]{1,0:T(4,128)} %bitcast.62, f32[4,192]{1,0:T(4,128)} %bitcast.66, s32[4,384]{1,0:T(4,128)} %bitcast.54, f32[4,384]{1,0:T(4,128)} %bitcast.58), custom_call_target="tpu_custom_call" | custom-call | flops 8000000000 | bytes 10000000 | tf_op jit(solution)/shard_map/aggregate2/pallas_call | solution.py:385
  12.6 11.7 %all-to-all-start = ((f32[64,48,128]{2,1,0:T(8,128)}), f32[64,48,128]{2,1,0:T(8,128)S(1)}, u32[]{:S(2)}, u32[]{:S(2)}) async-start(f32[64,48,128]{2,1,0:T(8,128)} %bitcast.51), calls=%async_computation | async-start | bytes 3145728 | tf_op jit(solution)/shard_map/all_to_all | solution.py:357
  24.5 0.1 copy.18
  24.6 0.7 mul.29.disp_ref
  25.3 0.1 copy.17
  25.4 0.1 reshape.71
  25.5 6.2 %operators.1 = (f32[5056,128]{1,0:T(8,128)}, f32[5056,128]{1,0:T(8,128)}) custom-call(s32[1]{0:T(128)} %bitcast.11.zh_ref, f32[11376,128]{1,0:T(8,128)} %bitcast.46), custom_call_target="tpu_custom_call" | custom-call | flops 1000000 | bytes 10000000 | tf_op jit(solution)/shard_map/operators/pallas_call | solution.py:389
  31.7 0.7 fusion.8.src_ref
  32.4 11.9 %aggregate1.1 = (f32[1536,128]{1,0:T(8,128)}, f32[8,192,384]{2,1,0:T(8,128)}, f32[8,192,384]{2,1,0:T(8,128)}) custom-call(s32[4,8]{1,0:T(4,128)} %oct_ref.7, f32[9216,128]{1,0:T(8,128)} %bitcast.71, f32[8,192,384]{2,1,0:T(8,128)} %angle_ref.3, s32[4,192]{1,0:T(4,128)} %bitcast.63, f32[4,192]{1,0:T(4,128)} %bitcast.67, s32[4,384]{1,0:T(4,128)} %bitcast.55, ...), custom_call_target="tpu_custom_call" | custom-call | flops 4000000000 | bytes 10000000 | tf_op jit(solution)/shard_map/aggregate1/pallas_call | solution.py:388
  44.2 4.5 %all-to-all-done = f32[64,48,128]{2,1,0:T(8,128)S(1)} async-done(((f32[64,48,128]{2,1,0:T(8,128)}), f32[64,48,128]{2,1,0:T(8,128)S(1)}, u32[]{:S(2)}, u32[]{:S(2)}) %all-to-all-start) | async-done | bytes 1572896 | tf_op jit(solution)/shard_map/all_to_all | solution.py:357
  48.7 6.0 %all-to-all-start.1 = ((f32[64,24,128]{2,1,0:T(8,128)}), f32[64,24,128]{2,1,0:T(8,128)S(1)}, u32[]{:S(2)}, u32[]{:S(2)}) async-start(f32[64,24,128]{2,1,0:T(8,128)} %bitcast.53), calls=%async_computation.1 | async-start | bytes 1572864 | tf_op jit(solution)/shard_map/all_to_all | solution.py:357
  54.7 17.4 %translate2.1 = f32[3072,128]{1,0:T(8,128)} custom-call(s32[8192]{0:T(1024)} %fusion.8.src_ref, s32[8192]{0:T(1024)} %mul.29.disp_ref, f32[3072,128]{1,0:T(8,128)} %bitcast.44, f32[3072,128]{1,0:T(8,128)} %collective-permute-done.other_ref, f32[5056,128]{1,0:T(8,128)} %get-tuple-element.30.t_ref), custom_call_target="tpu_custom_call" | custom-call | flops 100000000 | bytes 10000000 | tf_op jit(solution)/shard_map/translate2/pallas_call | solution.py:394
  72.1 10.3 %all-to-all-start.2 = ((f32[64,48,128]{2,1,0:T(8,128)}), f32[64,48,128]{2,1,0:T(8,128)S(1)}, u32[]{:S(2)}, u32[]{:S(2)}) async-start(f32[64,48,128]{2,1,0:T(8,128)} %bitcast.45), calls=%async_computation.2 | async-start | bytes 3145728 | tf_op jit(solution)/shard_map/all_to_all | solution.py:357
  82.4 0.1 collective-permute-start.1
  82.5 2.3 %collective-permute-done.1.other_ref = f32[1536,128]{1,0:T(8,128)S(1)} collective-permute-done((f32[1536,128]{1,0:T(8,128)S(1)}, f32[1536,128]{1,0:T(8,128)S(1)}, u32[]{:S(2)}, u32[]{:S(2)}) %collective-permute-start.1) | collective-permute-done | bytes 786464 | tf_op jit(solution)/shard_map/ppermute | solution.py:398
  84.8 0.9 copy-done.4
  85.7 16.8 %translate1.1 = f32[1536,128]{1,0:T(8,128)} custom-call(s32[8192]{0:T(1024)} %fusion.8.src_ref, s32[8192]{0:T(1024)} %mul.29.disp_ref, f32[1536,128]{1,0:T(8,128)} %bitcast.48, f32[1536,128]{1,0:T(8,128)} %copy-done.4, f32[5056,128]{1,0:T(8,128)} %get-tuple-element.33.t_ref), custom_call_target="tpu_custom_call" | custom-call | flops 100000000 | bytes 10000000 | tf_op jit(solution)/shard_map/translate1/pallas_call | solution.py:399
  102.5 4.5 %all-to-all-done.2 = f32[64,48,128]{2,1,0:T(8,128)S(1)} async-done(((f32[64,48,128]{2,1,0:T(8,128)}), f32[64,48,128]{2,1,0:T(8,128)S(1)}, u32[]{:S(2)}, u32[]{:S(2)}) %all-to-all-start.2) | async-done | bytes 1572896 | tf_op jit(solution)/shard_map/all_to_all | solution.py:357
  107.0 1.1 copy-done.3
  108.1 6.0 %all-to-all-start.3 = ((f32[64,24,128]{2,1,0:T(8,128)}), f32[64,24,128]{2,1,0:T(8,128)S(1)}, u32[]{:S(2)}, u32[]{:S(2)}) async-start(f32[64,24,128]{2,1,0:T(8,128)} %bitcast.49), calls=%async_computation.3 | async-start | bytes 1572864 | tf_op jit(solution)/shard_map/all_to_all | solution.py:357
  114.1 11.6 %disaggregate2.1.rest_0_ = f32[9216,128]{1,0:T(8,128)} custom-call(s32[4,8]{1,0:T(4,128)} %oct_ref.7, f32[3072,128]{1,0:T(8,128)} %bitcast.52, f32[8,192,384]{2,1,0:T(8,128)} %get-tuple-element.36.cos_ref, f32[8,192,384]{2,1,0:T(8,128)} %get-tuple-element.37.sin_ref, s32[4,192]{1,0:T(4,128)} %bitcast.64, f32[4,192]{1,0:T(4,128)} %bitcast.68, ...), custom_call_target="tpu_custom_call" | custom-call | flops 8000000000 | bytes 10000000 | tf_op jit(solution)/shard_map/disaggregate2/pallas_call | solution.py:403
  125.8 4.6 %all-to-all-done.3 = f32[64,24,128]{2,1,0:T(8,128)S(1)} async-done(((f32[64,24,128]{2,1,0:T(8,128)}), f32[64,24,128]{2,1,0:T(8,128)S(1)}, u32[]{:S(2)}, u32[]{:S(2)}) %all-to-all-start.3) | async-done | bytes 786464 | tf_op jit(solution)/shard_map/all_to_all | solution.py:357
  130.4 0.9 copy-done.2
  131.2 8.3 %disaggregate1.1 = f32[9216,128]{1,0:T(8,128)} custom-call(s32[4,8]{1,0:T(4,128)} %oct_ref.7, f32[1536,128]{1,0:T(8,128)} %bitcast.50, f32[8,192,384]{2,1,0:T(8,128)} %get-tuple-element.36.cos_ref, f32[8,192,384]{2,1,0:T(8,128)} %get-tuple-element.37.sin_ref, s32[4,192]{1,0:T(4,128)} %bitcast.65, f32[4,192]{1,0:T(4,128)} %bitcast.69, s32[4,384]{1,0:T(4,128)} %bitcast.57, ...), custom_call_target="tpu_custom_call" | custom-call | flops 4000000000 | bytes 10000000 | tf_op jit(solution)/shard_map/disaggregate1/pallas_call | solution.py:405
  (18 shorter events, 0.2 us)
Async XLA Ops:
  12.6 11.7 %copy-start.5 = (s32[512,32]{0,1:T(8,128)S(1)}, s32[512,32]{0,1:T(8,128)}, u32[]{:S(2)}) copy-start(s32[512,32]{0,1:T(8,128)} %param.17) | copy-start | bytes 196612
  12.6 11.7 %copy-start.6 = (s32[512,32]{0,1:T(8,128)S(1)}, s32[512,32]{0,1:T(8,128)}, u32[]{:S(2)}) copy-start(s32[512,32]{0,1:T(8,128)} %param.18) | copy-start | bytes 196612
  12.6 36.1 %all-to-all-start = ((f32[64,48,128]{2,1,0:T(8,128)}), f32[64,48,128]{2,1,0:T(8,128)S(1)}, u32[]{:S(2)}, u32[]{:S(2)}) async-start(f32[64,48,128]{2,1,0:T(8,128)} %bitcast.51), calls=%async_computation | async-start | bytes 3145728 | tf_op jit(solution)/shard_map/all_to_all | solution.py:357
  48.7 6.0 %copy-start = (f32[64,48,128]{2,1,0:T(8,128)}, f32[64,48,128]{2,1,0:T(8,128)S(1)}, u32[]{:S(2)}) copy-start(f32[64,48,128]{2,1,0:T(8,128)S(1)} %all-to-all-done) | copy-start | bytes 4718596
  48.7 6.0 %collective-permute-start = (f32[3072,128]{1,0:T(8,128)S(1)}, f32[3072,128]{1,0:T(8,128)}, u32[]{:S(2)}, u32[]{:S(2)}) collective-permute-start(f32[3072,128]{1,0:T(8,128)S(1)} %bitcast.43), channel_id=1, source_target_pairs={{0,32},{32,0},{1,33},{33,1},{2,34},{34,2},{3,35},{35,3},{4,36},{36... | collective-permute-start | bytes 4718600 | tf_op jit(solution)/shard_map/ppermute | solution.py:393
  48.7 23.4 %all-to-all-start.1 = ((f32[64,24,128]{2,1,0:T(8,128)}), f32[64,24,128]{2,1,0:T(8,128)S(1)}, u32[]{:S(2)}, u32[]{:S(2)}) async-start(f32[64,24,128]{2,1,0:T(8,128)} %bitcast.53), calls=%async_computation.1 | async-start | bytes 1572864 | tf_op jit(solution)/shard_map/all_to_all | solution.py:357
  72.1 12.7 %copy-start.1 = (f32[64,24,128]{2,1,0:T(8,128)}, f32[64,24,128]{2,1,0:T(8,128)S(1)}, u32[]{:S(2)}) copy-start(f32[64,24,128]{2,1,0:T(8,128)S(1)} %all-to-all-done.1) | copy-start | bytes 2359300
  72.1 34.9 %all-to-all-start.2 = ((f32[64,48,128]{2,1,0:T(8,128)}), f32[64,48,128]{2,1,0:T(8,128)S(1)}, u32[]{:S(2)}, u32[]{:S(2)}) async-start(f32[64,48,128]{2,1,0:T(8,128)} %bitcast.45), calls=%async_computation.2 | async-start | bytes 3145728 | tf_op jit(solution)/shard_map/all_to_all | solution.py:357
  82.4 2.4 %collective-permute-start.1 = (f32[1536,128]{1,0:T(8,128)S(1)}, f32[1536,128]{1,0:T(8,128)S(1)}, u32[]{:S(2)}, u32[]{:S(2)}) collective-permute-start(f32[1536,128]{1,0:T(8,128)S(1)} %bitcast.47), channel_id=1, source_target_pairs={{0,32},{32,0},{1,33},{33,1},{2,34},{34,2},{3,35},{35,3},{4,36},{36... | collective-permute-start | bytes 2359304 | tf_op jit(solution)/shard_map/ppermute | solution.py:398
  84.8 0.9 copy-start.4
  107.0 1.1 copy-start.3
  108.1 22.3 %all-to-all-start.3 = ((f32[64,24,128]{2,1,0:T(8,128)}), f32[64,24,128]{2,1,0:T(8,128)S(1)}, u32[]{:S(2)}, u32[]{:S(2)}) async-start(f32[64,24,128]{2,1,0:T(8,128)} %bitcast.49), calls=%async_computation.3 | async-start | bytes 1572864 | tf_op jit(solution)/shard_map/all_to_all | solution.py:357
  130.4 0.9 copy-start.2

commit v4 on v3

--- a/solution.py
+++ b/solution.py
@@ -12,6 +12,7 @@
 NDISP, NPART = 316, 32
 CHIPS = 64
 PARENTS = 4
+BOXES = CHIPS * PARENTS
 SLOT = 16
 FIRST, SECOND = (0, 1), (2,)
 F32, BF16 = jnp.float32, jnp.bfloat16
@@ -175,9 +176,8 @@
     def receiver(i, _):
         sums = None
         for q in range(NPART):
-            at = i * NPART + q
-            a = pl.multiple_of(src_ref[at], 8)
-            d = pl.multiple_of(disp_ref[at], 8)
+            a = pl.multiple_of(src_ref.at[pl.ds(q * BOXES, BOXES)][i], 8)
+            d = pl.multiple_of(disp_ref.at[pl.ds(q * BOXES, BOXES)][i], 8)
             s0, s1 = s_ref[pl.ds(a, 8), :], s_ref[pl.ds(a + 8, 8), :]
             t0 = t_ref[pl.ds(d, 8), :]
             if n == 1:
@@ -372,7 +372,7 @@
     stencils = (theta_index.T, theta_weight.T, phi_index.T, phi_weight.T)
 
     def mine(a):
-        return lax.dynamic_index_in_dim(a.reshape(2, 2, 128, NPART), core, 1, keepdims=False).reshape(-1)
+        return lax.dynamic_index_in_dim(a.T.reshape(NPART, 2, 2, 128), core, 2, keepdims=False).reshape(-1)
 
     src = mine(partner_src)
     holder, p = src // 4, src % 4

time: 140 us -> 136 us (0.971)
  Pallas kernels: 84.7 us -> 80.1 us
  waiting for transfers between devices: 15.9 us -> 19 us
  starting transfers between devices: 34.1 us -> 31.4 us
    all_to_all x4, waiting for transfers between devices: 13.6 us -> 16.7 us  [exchange(): lax.all_to_all(a.reshape(CHIPS, -1, 128), CHIP, 0, 0, tiled=True)]
    all_to_all x4, starting transfers between devices: 34 us -> 31.3 us  [exchange(): lax.all_to_all(a.reshape(CHIPS, -1, 128), CHIP, 0, 0, tiled=True)]
    pallas_call x1, Pallas kernels: 17.4 us -> 15.1 us  [local(): in1 = translate(FIRST)(src_at, disp_at, got1, other1, ops1)]
    pallas_call x1, Pallas kernels: 16.8 us -> 14.5 us  [local(): in2 = translate(SECOND)(src_at, disp_at, got2, other2, ops2)]
    unnamed x16 -> x14, local copies, waits for them, and re-layouts: 3.11 us -> 2.92 us
  transfers between devices with their start and end apart: 6 -> 6, of which waited for: 4 -> 5; matrix products, arithmetic and copies ran while one was open for 1% -> 1% of each run, Pallas kernels for 46% -> 44%
where the time goes in v4:
time: 136 us; the launch traced here: 135 us
  Pallas kernels  80.1 us (59%)
  starting transfers between devices  31.4 us (23%)
  waiting for transfers between devices  19 us (14%)
  local copies, waits for them, and re-layouts  3.03 us (2%)
  other arithmetic  1.36 us (1%)
    all_to_all x4, starting transfers between devices, exchange(): lax.all_to_all(a.reshape(CHIPS, -1, 128), CHIP, 0, 0, tiled=True)  31.3 us
    all_to_all x4, waiting for transfers between devices, exchange(): lax.all_to_all(a.reshape(CHIPS, -1, 128), CHIP, 0, 0, tiled=True)  16.7 us
    pallas_call x1, Pallas kernels, local(): in1 = translate(FIRST)(src_at, disp_at, got1, other1, ops1)  15.1 us
    pallas_call x1, Pallas kernels, local(): in2 = translate(SECOND)(src_at, disp_at, got2, other2, ops2)  14.5 us
    pallas_call x1, Pallas kernels, local(): out1, = aggregate(FIRST, False)(child_octant, x, shift_angle, *stencils)  12.6 us
    pallas_call x1, Pallas kernels, local(): aggregate(SECOND, True)(child_octant, x2, shift_angle, *stencils)  11.8 us
    pallas_call x1, Pallas kernels, local(): y = disaggregate(FIRST, 0)(child_octant, back1, cosine, sine, *stencils)  11.6 us
    pallas_call x1, Pallas kernels, local(): y = disaggregate(SECOND, 1)(child_octant, back2, cosine, sine, *stencils, y)  8.31 us
  transfers between devices with their start and end apart: 6, of which 5 were waited for; matrix products, arithmetic and copies ran while one was open for 1% of the time, Pallas kernels for 44%

profile of v4, /device:TPU:0, one launch (start us, length us, event | category | flops | bytes accessed | tf_op | source)
XLA Modules:
  0.0 135.0 jit_solution(5822183342141462082)
XLA Ops:
  0.0 12.6 %aggregate2.1 = f32[3072,128]{1,0:T(8,128)} custom-call(s32[4,8]{1,0:T(4,128)} %oct_ref.7, f32[9216,128]{1,0:T(8,128)} %bitcast.67, f32[8,192,384]{2,1,0:T(8,128)} %angle_ref.3, s32[4,192]{1,0:T(4,128)} %bitcast.59, f32[4,192]{1,0:T(4,128)} %bitcast.63, s32[4,384]{1,0:T(4,128)} %bitcast.51, f32[4,384]{1,0:T(4,128)} %bitcast.55), custom_call_target="tpu_custom_call" | custom-call | flops 8000000000 | bytes 10000000 | tf_op jit(solution)/shard_map/aggregate2/pallas_call | solution.py:385
  12.6 11.7 %all-to-all-start = ((f32[64,48,128]{2,1,0:T(8,128)}), f32[64,48,128]{2,1,0:T(8,128)S(1)}, u32[]{:S(2)}, u32[]{:S(2)}) async-start(f32[64,48,128]{2,1,0:T(8,128)} %bitcast.43), calls=%async_computation | async-start | bytes 3145728 | tf_op jit(solution)/shard_map/all_to_all | solution.py:357
  24.4 6.2 %operators.1 = (f32[5056,128]{1,0:T(8,128)}, f32[5056,128]{1,0:T(8,128)}) custom-call(s32[1]{0:T(128)} %bitcast.11.zh_ref, f32[11376,128]{1,0:T(8,128)} %bitcast.38), custom_call_target="tpu_custom_call" | custom-call | flops 1000000 | bytes 10000000 | tf_op jit(solution)/shard_map/operators/pallas_call | solution.py:389
  30.6 0.7 dynamic-slice_multiply_fusion
  31.3 0.7 fusion.8.src_ref
  32.0 11.8 %aggregate1.1 = (f32[1536,128]{1,0:T(8,128)}, f32[8,192,384]{2,1,0:T(8,128)}, f32[8,192,384]{2,1,0:T(8,128)}) custom-call(s32[4,8]{1,0:T(4,128)} %oct_ref.7, f32[9216,128]{1,0:T(8,128)} %bitcast.68, f32[8,192,384]{2,1,0:T(8,128)} %angle_ref.3, s32[4,192]{1,0:T(4,128)} %bitcast.60, f32[4,192]{1,0:T(4,128)} %bitcast.64, s32[4,384]{1,0:T(4,128)} %bitcast.52, ...), custom_call_target="tpu_custom_call" | custom-call | flops 4000000000 | bytes 10000000 | tf_op jit(solution)/shard_map/aggregate1/pallas_call | solution.py:388
  43.8 4.9 %all-to-all-done = f32[64,48,128]{2,1,0:T(8,128)S(1)} async-done(((f32[64,48,128]{2,1,0:T(8,128)}), f32[64,48,128]{2,1,0:T(8,128)S(1)}, u32[]{:S(2)}, u32[]{:S(2)}) %all-to-all-start) | async-done | bytes 1572896 | tf_op jit(solution)/shard_map/all_to_all | solution.py:357
  48.7 0.0 collective-permute-start
  48.7 5.5 %all-to-all-start.1 = ((f32[64,24,128]{2,1,0:T(8,128)}), f32[64,24,128]{2,1,0:T(8,128)S(1)}, u32[]{:S(2)}, u32[]{:S(2)}) async-start(f32[64,24,128]{2,1,0:T(8,128)} %bitcast.45), calls=%async_computation.1 | async-start | bytes 1572864 | tf_op jit(solution)/shard_map/all_to_all | solution.py:357
  54.3 0.0 collective-permute-done.other_ref
  54.3 15.1 %translate2.1 = f32[3072,128]{1,0:T(8,128)} custom-call(s32[8192]{0:T(1024)} %fusion.8.src_ref, s32[8192]{0:T(1024)} %bitcast.46, f32[3072,128]{1,0:T(8,128)} %bitcast.36, f32[3072,128]{1,0:T(8,128)} %collective-permute-done.other_ref, f32[5056,128]{1,0:T(8,128)} %get-tuple-element.30.t_ref), custom_call_target="tpu_custom_call" | custom-call | flops 100000000 | bytes 10000000 | tf_op jit(solution)/shard_map/translate2/pallas_call | solution.py:394
  69.4 1.7 %all-to-all-done.1 = f32[64,24,128]{2,1,0:T(8,128)S(1)} async-done(((f32[64,24,128]{2,1,0:T(8,128)}), f32[64,24,128]{2,1,0:T(8,128)S(1)}, u32[]{:S(2)}, u32[]{:S(2)}) %all-to-all-start.1) | async-done | bytes 786464 | tf_op jit(solution)/shard_map/all_to_all | solution.py:357
  71.1 8.7 %all-to-all-start.2 = ((f32[64,48,128]{2,1,0:T(8,128)}), f32[64,48,128]{2,1,0:T(8,128)S(1)}, u32[]{:S(2)}, u32[]{:S(2)}) async-start(f32[64,48,128]{2,1,0:T(8,128)} %bitcast.37), calls=%async_computation.2 | async-start | bytes 3145728 | tf_op jit(solution)/shard_map/all_to_all | solution.py:357
  79.7 0.1 collective-permute-start.1
  79.8 2.3 %collective-permute-done.1.other_ref = f32[1536,128]{1,0:T(8,128)S(1)} collective-permute-done((f32[1536,128]{1,0:T(8,128)S(1)}, f32[1536,128]{1,0:T(8,128)S(1)}, u32[]{:S(2)}, u32[]{:S(2)}) %collective-permute-start.1) | collective-permute-done | bytes 786464 | tf_op jit(solution)/shard_map/ppermute | solution.py:398
  82.1 0.9 copy-done.4
  83.0 14.5 %translate1.1 = f32[1536,128]{1,0:T(8,128)} custom-call(s32[8192]{0:T(1024)} %fusion.8.src_ref, s32[8192]{0:T(1024)} %bitcast.47, f32[1536,128]{1,0:T(8,128)} %bitcast.40, f32[1536,128]{1,0:T(8,128)} %copy-done.4, f32[5056,128]{1,0:T(8,128)} %get-tuple-element.33.t_ref), custom_call_target="tpu_custom_call" | custom-call | flops 100000000 | bytes 10000000 | tf_op jit(solution)/shard_map/translate1/pallas_call | solution.py:399
  97.5 6.8 %all-to-all-done.2 = f32[64,48,128]{2,1,0:T(8,128)S(1)} async-done(((f32[64,48,128]{2,1,0:T(8,128)}), f32[64,48,128]{2,1,0:T(8,128)S(1)}, u32[]{:S(2)}, u32[]{:S(2)}) %all-to-all-start.2) | async-done | bytes 1572896 | tf_op jit(solution)/shard_map/all_to_all | solution.py:357
  104.3 1.1 copy-done.3
  105.4 5.4 %all-to-all-start.3 = ((f32[64,24,128]{2,1,0:T(8,128)}), f32[64,24,128]{2,1,0:T(8,128)S(1)}, u32[]{:S(2)}, u32[]{:S(2)}) async-start(f32[64,24,128]{2,1,0:T(8,128)} %bitcast.41), calls=%async_computation.3 | async-start | bytes 1572864 | tf_op jit(solution)/shard_map/all_to_all | solution.py:357
  110.8 11.6 %disaggregate2.1.rest_0_ = f32[9216,128]{1,0:T(8,128)} custom-call(s32[4,8]{1,0:T(4,128)} %oct_ref.7, f32[3072,128]{1,0:T(8,128)} %bitcast.44, f32[8,192,384]{2,1,0:T(8,128)} %get-tuple-element.36.cos_ref, f32[8,192,384]{2,1,0:T(8,128)} %get-tuple-element.37.sin_ref, s32[4,192]{1,0:T(4,128)} %bitcast.61, f32[4,192]{1,0:T(4,128)} %bitcast.65, ...), custom_call_target="tpu_custom_call" | custom-call | flops 8000000000 | bytes 10000000 | tf_op jit(solution)/shard_map/disaggregate2/pallas_call | solution.py:403
  122.4 3.4 %all-to-all-done.3 = f32[64,24,128]{2,1,0:T(8,128)S(1)} async-done(((f32[64,24,128]{2,1,0:T(8,128)}), f32[64,24,128]{2,1,0:T(8,128)S(1)}, u32[]{:S(2)}, u32[]{:S(2)}) %all-to-all-start.3) | async-done | bytes 786464 | tf_op jit(solution)/shard_map/all_to_all | solution.py:357
  125.8 0.9 copy-done.2
  126.7 8.3 %disaggregate1.1 = f32[9216,128]{1,0:T(8,128)} custom-call(s32[4,8]{1,0:T(4,128)} %oct_ref.7, f32[1536,128]{1,0:T(8,128)} %bitcast.42, f32[8,192,384]{2,1,0:T(8,128)} %get-tuple-element.36.cos_ref, f32[8,192,384]{2,1,0:T(8,128)} %get-tuple-element.37.sin_ref, s32[4,192]{1,0:T(4,128)} %bitcast.62, f32[4,192]{1,0:T(4,128)} %bitcast.66, s32[4,384]{1,0:T(4,128)} %bitcast.54, ...), custom_call_target="tpu_custom_call" | custom-call | flops 4000000000 | bytes 10000000 | tf_op jit(solution)/shard_map/disaggregate1/pallas_call | solution.py:405
  (14 shorter events, 0.1 us)
Async XLA Ops:
  12.6 11.7 %copy-start.5 = (s32[512,32]{0,1:T(8,128)S(1)}, s32[512,32]{0,1:T(8,128)}, u32[]{:S(2)}) copy-start(s32[512,32]{0,1:T(8,128)} %param.17) | copy-start | bytes 196612
  12.6 11.7 %copy-start.6 = (s32[512,32]{0,1:T(8,128)S(1)}, s32[512,32]{0,1:T(8,128)}, u32[]{:S(2)}) copy-start(s32[512,32]{0,1:T(8,128)} %param.18) | copy-start | bytes 196612
  12.6 36.1 %all-to-all-start = ((f32[64,48,128]{2,1,0:T(8,128)}), f32[64,48,128]{2,1,0:T(8,128)S(1)}, u32[]{:S(2)}, u32[]{:S(2)}) async-start(f32[64,48,128]{2,1,0:T(8,128)} %bitcast.43), calls=%async_computation | async-start | bytes 3145728 | tf_op jit(solution)/shard_map/all_to_all | solution.py:357
  48.7 5.6 %copy-start = (f32[64,48,128]{2,1,0:T(8,128)}, f32[64,48,128]{2,1,0:T(8,128)S(1)}, u32[]{:S(2)}) copy-start(f32[64,48,128]{2,1,0:T(8,128)S(1)} %all-to-all-done) | copy-start | bytes 4718596
  48.7 5.6 %collective-permute-start = (f32[3072,128]{1,0:T(8,128)S(1)}, f32[3072,128]{1,0:T(8,128)}, u32[]{:S(2)}, u32[]{:S(2)}) collective-permute-start(f32[3072,128]{1,0:T(8,128)S(1)} %bitcast.35), channel_id=1, source_target_pairs={{0,32},{32,0},{1,33},{33,1},{2,34},{34,2},{3,35},{35,3},{4,36},{36... | collective-permute-start | bytes 4718600 | tf_op jit(solution)/shard_map/ppermute | solution.py:393
  48.7 22.3 %all-to-all-start.1 = ((f32[64,24,128]{2,1,0:T(8,128)}), f32[64,24,128]{2,1,0:T(8,128)S(1)}, u32[]{:S(2)}, u32[]{:S(2)}) async-start(f32[64,24,128]{2,1,0:T(8,128)} %bitcast.45), calls=%async_computation.1 | async-start | bytes 1572864 | tf_op jit(solution)/shard_map/all_to_all | solution.py:357
  71.1 11.1 %copy-start.1 = (f32[64,24,128]{2,1,0:T(8,128)}, f32[64,24,128]{2,1,0:T(8,128)S(1)}, u32[]{:S(2)}) copy-start(f32[64,24,128]{2,1,0:T(8,128)S(1)} %all-to-all-done.1) | copy-start | bytes 2359300
  71.1 33.2 %all-to-all-start.2 = ((f32[64,48,128]{2,1,0:T(8,128)}), f32[64,48,128]{2,1,0:T(8,128)S(1)}, u32[]{:S(2)}, u32[]{:S(2)}) async-start(f32[64,48,128]{2,1,0:T(8,128)} %bitcast.37), calls=%async_computation.2 | async-start | bytes 3145728 | tf_op jit(solution)/shard_map/all_to_all | solution.py:357
  79.7 2.4 %collective-permute-start.1 = (f32[1536,128]{1,0:T(8,128)S(1)}, f32[1536,128]{1,0:T(8,128)S(1)}, u32[]{:S(2)}, u32[]{:S(2)}) collective-permute-start(f32[1536,128]{1,0:T(8,128)S(1)} %bitcast.39), channel_id=1, source_target_pairs={{0,32},{32,0},{1,33},{33,1},{2,34},{34,2},{3,35},{35,3},{4,36},{36... | collective-permute-start | bytes 2359304 | tf_op jit(solution)/shard_map/ppermute | solution.py:398
  82.1 0.9 copy-start.4
  104.3 1.1 copy-start.3
  105.4 20.4 %all-to-all-start.3 = ((f32[64,24,128]{2,1,0:T(8,128)}), f32[64,24,128]{2,1,0:T(8,128)S(1)}, u32[]{:S(2)}, u32[]{:S(2)}) async-start(f32[64,24,128]{2,1,0:T(8,128)} %bitcast.41), calls=%async_computation.3 | async-start | bytes 1572864 | tf_op jit(solution)/shard_map/all_to_all | solution.py:357
  125.8 0.9 copy-start.2

commit v5 on v4

--- a/solution.py
+++ b/solution.py
@@ -259,7 +259,8 @@
 VMEM = pl.BlockSpec(memory_space=pltpu.VMEM)
 SMEM = pl.BlockSpec(memory_space=pltpu.SMEM)
 STENCILS = [whole((4, NT2)), whole((4, NT2)), whole((4, NP2)), whole((4, NP2))]
-PARAMS = pltpu.CompilerParams(vmem_limit_bytes=60 * 2**20)
+PARAMS = pltpu.CompilerParams(vmem_limit_bytes=52 * 2**20)
+ROOMY = pltpu.CompilerParams(vmem_limit_bytes=60 * 2**20)
 CHILDREN = pl.BlockSpec((8 * 288, 128), lambda p: (p, 0))
 
 
@@ -300,7 +301,7 @@
             pltpu.VMEM((8, 288, 256 * n), BF16),
             pltpu.VMEM((2 * n, NT2, 128), F32),
         ],
-        compiler_params=PARAMS,
+        compiler_params=ROOMY,
         cost_estimate=cost(n * 4 * 10**9, 10**7),
         name=f"aggregate{n}",
     )
@@ -312,7 +313,7 @@
         in_specs=[SMEM, VMEM],
         out_specs=[VMEM, VMEM],
         out_shape=[jax.ShapeDtypeStruct((NDISP * SLOT, 128), F32)] * 2,
-        compiler_params=PARAMS,
+        compiler_params=ROOMY,
         cost_estimate=cost(10**6, 10**7),
         name="operators",
     )

time: 136 us -> 133 us (0.978)
  local copies, waits for them, and re-layouts: 3.03 us -> 1.04 us
  waiting for transfers between devices: 19 us -> 20.7 us
    unnamed x14 -> x18, local copies, waits for them, and re-layouts: 2.92 us -> 0.92 us
    all_to_all x4, waiting for transfers between devices: 16.7 us -> 18.5 us  [exchange(): lax.all_to_all(a.reshape(CHIPS, -1, 128), CHIP, 0, 0, tiled=True)]
  transfers between devices with their start and end apart: 6 -> 6, of which waited for: 5 -> 5; matrix products, arithmetic and copies ran while one was open for 1% -> 0% of each run, Pallas kernels for 44% -> 44%
where the time goes in v5:
time: 133 us; the launch traced here: 132 us
  Pallas kernels  79.3 us (60%)
  starting transfers between devices  31 us (23%)
  waiting for transfers between devices  20.7 us (16%)
    all_to_all x4, starting transfers between devices, exchange(): lax.all_to_all(a.reshape(CHIPS, -1, 128), CHIP, 0, 0, tiled=True)  30.9 us
    all_to_all x4, waiting for transfers between devices, exchange(): lax.all_to_all(a.reshape(CHIPS, -1, 128), CHIP, 0, 0, tiled=True)  18.5 us
    pallas_call x1, Pallas kernels, local(): in1 = translate(FIRST)(src_at, disp_at, got1, other1, ops1)  15.2 us
    pallas_call x1, Pallas kernels, local(): in2 = translate(SECOND)(src_at, disp_at, got2, other2, ops2)  14.3 us
    pallas_call x1, Pallas kernels, local(): out1, = aggregate(FIRST, False)(child_octant, x, shift_angle, *stencils)  12.7 us
    pallas_call x1, Pallas kernels, local(): aggregate(SECOND, True)(child_octant, x2, shift_angle, *stencils)  11.9 us
    pallas_call x1, Pallas kernels, local(): y = disaggregate(FIRST, 0)(child_octant, back1, cosine, sine, *stencils)  11.1 us
    pallas_call x1, Pallas kernels, local(): y = disaggregate(SECOND, 1)(child_octant, back2, cosine, sine, *stencils, y)  8.03 us
  transfers between devices with their start and end apart: 6, of which 5 were waited for; matrix products, arithmetic and copies ran while one was open for 0% of the time, Pallas kernels for 44%

profile of v5, /device:TPU:0, one launch (start us, length us, event | category | flops | bytes accessed | tf_op | source)
XLA Modules:
  0.0 132.5 jit_solution(12220883668801910769)
XLA Ops:
  0.0 12.7 %aggregate2.1 = f32[3072,128]{1,0:T(8,128)} custom-call(s32[4,8]{1,0:T(4,128)} %oct_ref.7, f32[9216,128]{1,0:T(8,128)} %bitcast.65, f32[8,192,384]{2,1,0:T(8,128)} %angle_ref.3, s32[4,192]{1,0:T(4,128)} %bitcast.49, f32[4,192]{1,0:T(4,128)} %bitcast.53, s32[4,384]{1,0:T(4,128)} %bitcast.41, f32[4,384]{1,0:T(4,128)} %bitcast.45), custom_call_target="tpu_custom_call" | custom-call | flops 8000000000 | bytes 10000000 | tf_op jit(solution)/shard_map/aggregate2/pallas_call | solution.py:386
  12.7 11.7 %all-to-all-start = ((f32[64,48,128]{2,1,0:T(8,128)}), f32[64,48,128]{2,1,0:T(8,128)S(1)}, u32[]{:S(2)}, u32[]{:S(2)}) async-start(f32[64,48,128]{2,1,0:T(8,128)} %bitcast.60), calls=%async_computation | async-start | bytes 3145728 | tf_op jit(solution)/shard_map/all_to_all | solution.py:358
  24.5 6.2 %operators.1 = (f32[5056,128]{1,0:T(8,128)}, f32[5056,128]{1,0:T(8,128)}) custom-call(s32[1]{0:T(128)} %bitcast.11.zh_ref, f32[11376,128]{1,0:T(8,128)} %bitcast.59), custom_call_target="tpu_custom_call" | custom-call | flops 1000000 | bytes 10000000 | tf_op jit(solution)/shard_map/operators/pallas_call | solution.py:390
  30.8 0.1 fusion.8.src_ref
  30.9 11.9 %aggregate1.1 = (f32[1536,128]{1,0:T(8,128)}, f32[8,192,384]{2,1,0:T(8,128)}, f32[8,192,384]{2,1,0:T(8,128)}) custom-call(s32[4,8]{1,0:T(4,128)} %oct_ref.7, f32[9216,128]{1,0:T(8,128)} %bitcast.66, f32[8,192,384]{2,1,0:T(8,128)} %angle_ref.3, s32[4,192]{1,0:T(4,128)} %bitcast.50, f32[4,192]{1,0:T(4,128)} %bitcast.54, s32[4,384]{1,0:T(4,128)} %bitcast.42, ...), custom_call_target="tpu_custom_call" | custom-call | flops 4000000000 | bytes 10000000 | tf_op jit(solution)/shard_map/aggregate1/pallas_call | solution.py:389
  42.7 6.0 %all-to-all-done = f32[64,48,128]{2,1,0:T(8,128)S(1)} async-done(((f32[64,48,128]{2,1,0:T(8,128)}), f32[64,48,128]{2,1,0:T(8,128)S(1)}, u32[]{:S(2)}, u32[]{:S(2)}) %all-to-all-start) | async-done | bytes 1572896 | tf_op jit(solution)/shard_map/all_to_all | solution.py:358
  48.8 5.1 %all-to-all-start.1 = ((f32[64,24,128]{2,1,0:T(8,128)}), f32[64,24,128]{2,1,0:T(8,128)S(1)}, u32[]{:S(2)}, u32[]{:S(2)}) async-start(f32[64,24,128]{2,1,0:T(8,128)} %bitcast.61), calls=%async_computation.1 | async-start | bytes 1572864 | tf_op jit(solution)/shard_map/all_to_all | solution.py:358
  53.9 15.2 %translate2.1 = f32[3072,128]{1,0:T(8,128)} custom-call(s32[8192]{0:T(1024)S(1)} %fusion.8.src_ref, s32[8192]{0:T(1024)S(1)} %bitcast.39, f32[3072,128]{1,0:T(8,128)} %bitcast.58, f32[3072,128]{1,0:T(8,128)} %collective-permute-done.other_ref, f32[5056,128]{1,0:T(8,128)} %get-tuple-element.30.t_ref), custom_call_target="tpu_custom_call" | custom-call | flops 100000000 | bytes 10000000 | tf_op jit(solution)/shard_map/translate2/pallas_call | solution.py:395
  69.1 1.6 %all-to-all-done.1 = f32[64,24,128]{2,1,0:T(8,128)S(1)} async-done(((f32[64,24,128]{2,1,0:T(8,128)}), f32[64,24,128]{2,1,0:T(8,128)S(1)}, u32[]{:S(2)}, u32[]{:S(2)}) %all-to-all-start.1) | async-done | bytes 786464 | tf_op jit(solution)/shard_map/all_to_all | solution.py:358
  70.7 8.7 %all-to-all-start.2 = ((f32[64,48,128]{2,1,0:T(8,128)}), f32[64,48,128]{2,1,0:T(8,128)S(1)}, u32[]{:S(2)}, u32[]{:S(2)}) async-start(f32[64,48,128]{2,1,0:T(8,128)} %bitcast.23), calls=%async_computation.2 | async-start | bytes 3145728 | tf_op jit(solution)/shard_map/all_to_all | solution.py:358
  79.5 0.0 copy-start
  79.5 0.0 copy-start.1
  79.5 0.0 copy-start.2
  79.5 0.0 copy-start.3
  79.5 0.0 copy-start.4
  79.5 0.1 collective-permute-start.1
  79.6 2.3 %collective-permute-done.1.other_ref = f32[1536,128]{1,0:T(8,128)S(1)} collective-permute-done((f32[1536,128]{1,0:T(8,128)S(1)}, f32[1536,128]{1,0:T(8,128)S(1)}, u32[]{:S(2)}, u32[]{:S(2)}) %collective-permute-start.1) | collective-permute-done | bytes 786464 | tf_op jit(solution)/shard_map/ppermute | solution.py:399
  81.9 0.9 copy-done.6
  82.8 14.3 %translate1.1 = f32[1536,128]{1,0:T(8,128)} custom-call(s32[8192]{0:T(1024)S(1)} %fusion.8.src_ref, s32[8192]{0:T(1024)S(1)} %bitcast.40, f32[1536,128]{1,0:T(8,128)S(1)} %bitcast.36, f32[1536,128]{1,0:T(8,128)} %copy-done.6, f32[5056,128]{1,0:T(8,128)} %get-tuple-element.33.t_ref), custom_call_target="tpu_custom_call" | custom-call | flops 100000000 | bytes 10000000 | tf_op jit(solution)/shard_map/translate1/pallas_call | solution.py:400
  97.0 7.0 %all-to-all-done.2 = f32[64,48,128]{2,1,0:T(8,128)S(1)} async-done(((f32[64,48,128]{2,1,0:T(8,128)}), f32[64,48,128]{2,1,0:T(8,128)S(1)}, u32[]{:S(2)}, u32[]{:S(2)}) %all-to-all-start.2) | async-done | bytes 1572896 | tf_op jit(solution)/shard_map/all_to_all | solution.py:358
  104.0 5.4 %all-to-all-start.3 = ((f32[64,24,128]{2,1,0:T(8,128)}), f32[64,24,128]{2,1,0:T(8,128)S(1)}, u32[]{:S(2)}, u32[]{:S(2)}) async-start(f32[64,24,128]{2,1,0:T(8,128)} %bitcast.25), calls=%async_computation.3 | async-start | bytes 1572864 | tf_op jit(solution)/shard_map/all_to_all | solution.py:358
  109.5 11.1 %disaggregate2.1.rest_0_ = f32[9216,128]{1,0:T(8,128)} custom-call(s32[4,8]{1,0:T(4,128)S(1)} %copy-done.4, f32[3072,128]{1,0:T(8,128)S(1)} %bitcast.38, f32[8,192,384]{2,1,0:T(8,128)} %get-tuple-element.36.cos_ref, f32[8,192,384]{2,1,0:T(8,128)} %get-tuple-element.37.sin_ref, s32[4,192]{1,0:T(4,128)S(1)} %bitcast.51, f32[4,192]{1,0:T(4,128)S(1)} %bitcast.55, ...), custom_call_target="tpu_custom_call" | custom-call | flops 8000000000 | bytes 10000000 | tf_op jit(solution)/shard_map/disaggregate2/pallas_call | solution.py:404
  120.6 3.8 %all-to-all-done.3 = f32[64,24,128]{2,1,0:T(8,128)S(1)} async-done(((f32[64,24,128]{2,1,0:T(8,128)}), f32[64,24,128]{2,1,0:T(8,128)S(1)}, u32[]{:S(2)}, u32[]{:S(2)}) %all-to-all-start.3) | async-done | bytes 786464 | tf_op jit(solution)/shard_map/all_to_all | solution.py:358
  124.4 8.0 %disaggregate1.1 = f32[9216,128]{1,0:T(8,128)} custom-call(s32[4,8]{1,0:T(4,128)S(1)} %copy-done.4, f32[1536,128]{1,0:T(8,128)S(1)} %bitcast.37, f32[8,192,384]{2,1,0:T(8,128)} %get-tuple-element.36.cos_ref, f32[8,192,384]{2,1,0:T(8,128)} %get-tuple-element.37.sin_ref, s32[4,192]{1,0:T(4,128)S(1)} %bitcast.52, f32[4,192]{1,0:T(4,128)S(1)} %bitcast.56, ...), custom_call_target="tpu_custom_call" | custom-call | flops 4000000000 | bytes 10000000 | tf_op jit(solution)/shard_map/disaggregate1/pallas_call | solution.py:406
  (18 shorter events, 0.2 us)
Async XLA Ops:
  12.7 11.7 %copy-start.7 = (s32[512,32]{0,1:T(8,128)S(1)}, s32[512,32]{0,1:T(8,128)}, u32[]{:S(2)}) copy-start(s32[512,32]{0,1:T(8,128)} %param.17) | copy-start | bytes 196612
  12.7 11.7 %copy-start.8 = (s32[512,32]{0,1:T(8,128)S(1)}, s32[512,32]{0,1:T(8,128)}, u32[]{:S(2)}) copy-start(s32[512,32]{0,1:T(8,128)} %param.18) | copy-start | bytes 196612
  12.7 36.1 %all-to-all-start = ((f32[64,48,128]{2,1,0:T(8,128)}), f32[64,48,128]{2,1,0:T(8,128)S(1)}, u32[]{:S(2)}, u32[]{:S(2)}) async-start(f32[64,48,128]{2,1,0:T(8,128)} %bitcast.60), calls=%async_computation | async-start | bytes 3145728 | tf_op jit(solution)/shard_map/all_to_all | solution.py:358
  48.8 5.2 %copy-start.5 = (f32[64,48,128]{2,1,0:T(8,128)}, f32[64,48,128]{2,1,0:T(8,128)S(1)}, u32[]{:S(2)}) copy-start(f32[64,48,128]{2,1,0:T(8,128)S(1)} %all-to-all-done) | copy-start | bytes 4718596
  48.8 5.2 %collective-permute-start = (f32[3072,128]{1,0:T(8,128)S(1)}, f32[3072,128]{1,0:T(8,128)}, u32[]{:S(2)}, u32[]{:S(2)}) collective-permute-start(f32[3072,128]{1,0:T(8,128)S(1)} %bitcast.57), channel_id=1, source_target_pairs={{0,32},{32,0},{1,33},{33,1},{2,34},{34,2},{3,35},{35,3},{4,36},{36... | collective-permute-start | bytes 4718600 | tf_op jit(solution)/shard_map/ppermute | solution.py:394
  48.8 21.9 %all-to-all-start.1 = ((f32[64,24,128]{2,1,0:T(8,128)}), f32[64,24,128]{2,1,0:T(8,128)S(1)}, u32[]{:S(2)}, u32[]{:S(2)}) async-start(f32[64,24,128]{2,1,0:T(8,128)} %bitcast.61), calls=%async_computation.1 | async-start | bytes 1572864 | tf_op jit(solution)/shard_map/all_to_all | solution.py:358
  70.7 33.3 %all-to-all-start.2 = ((f32[64,48,128]{2,1,0:T(8,128)}), f32[64,48,128]{2,1,0:T(8,128)S(1)}, u32[]{:S(2)}, u32[]{:S(2)}) async-start(f32[64,48,128]{2,1,0:T(8,128)} %bitcast.23), calls=%async_computation.2 | async-start | bytes 3145728 | tf_op jit(solution)/shard_map/all_to_all | solution.py:358
  79.5 29.9 %copy-start = (s32[384,4]{0,1:T(4,128)S(1)}, s32[384,4]{0,1:T(4,128)}, u32[]{:S(2)}) copy-start(s32[384,4]{0,1:T(4,128)} %param.14) | copy-start | bytes 18436
  79.5 29.9 %copy-start.1 = (f32[384,4]{0,1:T(4,128)S(1)}, f32[384,4]{0,1:T(4,128)}, u32[]{:S(2)}) copy-start(f32[384,4]{0,1:T(4,128)} %param.15) | copy-start | bytes 18436
  79.5 29.9 %copy-start.2 = (s32[192,4]{0,1:T(4,128)S(1)}, s32[192,4]{0,1:T(4,128)}, u32[]{:S(2)}) copy-start(s32[192,4]{0,1:T(4,128)} %param.12) | copy-start | bytes 9220
  79.5 29.9 %copy-start.3 = (f32[192,4]{0,1:T(4,128)S(1)}, f32[192,4]{0,1:T(4,128)}, u32[]{:S(2)}) copy-start(f32[192,4]{0,1:T(4,128)} %param.13) | copy-start | bytes 9220
  79.5 29.9 %copy-start.4 = (s32[4,8]{1,0:T(4,128)S(1)}, s32[4,8]{1,0:T(4,128)}, u32[]{:S(2)}) copy-start(s32[4,8]{1,0:T(4,128)} %oct_ref.7) | copy-start | bytes 388
  79.5 2.4 %collective-permute-start.1 = (f32[1536,128]{1,0:T(8,128)S(1)}, f32[1536,128]{1,0:T(8,128)S(1)}, u32[]{:S(2)}, u32[]{:S(2)}) collective-permute-start(f32[1536,128]{1,0:T(8,128)S(1)} %bitcast.35), channel_id=1, source_target_pairs={{0,32},{32,0},{1,33},{33,1},{2,34},{34,2},{3,35},{35,3},{4,36},{36... | collective-permute-start | bytes 2359304 | tf_op jit(solution)/shard_map/ppermute | solution.py:399
  81.9 0.9 copy-start.6
  104.0 20.4 %all-to-all-start.3 = ((f32[64,24,128]{2,1,0:T(8,128)}), f32[64,24,128]{2,1,0:T(8,128)S(1)}, u32[]{:S(2)}, u32[]{:S(2)}) async-start(f32[64,24,128]{2,1,0:T(8,128)} %bitcast.25), calls=%async_computation.3 | async-start | bytes 1572864 | tf_op jit(solution)/shard_map/all_to_all | solution.py:358

commit v6 on v5

--- a/solution.py
+++ b/solution.py
@@ -26,7 +26,7 @@
     return [float(v) for v in np.linalg.lstsq(a, fn(h), rcond=None)[0]]
 
 
-SIN = fit(np.sin, (1, 3, 5, 7, 9, 11))
+SIN = fit(np.sin, (1, 3, 5, 7, 9))
 COS = fit(np.cos, (0, 2, 4, 6, 8, 10))
 
 
@@ -111,7 +111,7 @@
                     r = (kk * 2 + part) * 48
                     for j in range(n):
                         col = j * 256 + part * 128
-                        for base, v in ((0, yh), (96, yl), (192, yh)):
+                        for base, v in ((0, yh), (96, yl)):
                             y3_ref[m // 96 + kk, base + odd * 48 : base + odd * 48 + 48, col : col + 128] = v[
                                 r : r + 48, j * 128 : j * 128 + 128
                             ]
@@ -119,7 +119,8 @@
     for k in range(8):
         o = oct_ref[p, k]
         for j in range(n):
-            f = dot(t3_ref[...], y3_ref[k, :, j * 256 : j * 256 + 256])
+            y = y3_ref[k, :, j * 256 : j * 256 + 256]
+            f = dot(t3_ref[:, :192], y) + dot(t3_ref[:, 192:], y[:96])
             re, im = f[:, :128], f[:, 128:]
             at = (first + j) * 128
             c = cos_ref[o, :, at : at + 128]
@@ -144,12 +145,11 @@
     half = zh_ref[0] * 18
 
     def one(d, _):
-        for ref, tiles in ((first_ref, FIRST), (second_ref, SECOND)):
-            gap = 8 if len(tiles) == 2 else 3
+        for ref, tiles, slot, gap in ((first_ref, FIRST, SLOT, 8), (second_ref, SECOND, SLOT // 2, 3)):
             for part in range(2):
                 for jj, j in enumerate(tiles):
                     v = t_ref[pl.ds(d * 36 + half + j * 2 + part, 3, stride=6), :]
-                    ref[pl.ds(d * SLOT + part * gap + jj * 3, 3), :] = v
+                    ref[pl.ds(d * slot + part * gap + jj * 3, 3), :] = v
         return 0
 
     lax.fori_loop(0, NDISP, one, 0, unroll=4)
@@ -171,7 +171,7 @@
                     s_ref[pl.ds(to + 11, half), :] = re
         return 0
 
-    lax.fori_loop(0, CHIPS, lay, 0, unroll=2)
+    lax.fori_loop(0, CHIPS, lay, 0, unroll=4)
 
     def receiver(i, _):
         sums = None
@@ -195,7 +195,7 @@
         out_ref[pl.ds(to + half, half), :] = im
         return 0
 
-    lax.fori_loop(0, CHIPS * PARENTS, receiver, 0, unroll=2)
+    lax.fori_loop(0, CHIPS * PARENTS, receiver, 0, unroll=4)
 
 
 def disaggregate_kernel(tiles, oct_ref, x_ref, cos_ref, sin_ref, ti_ref, tw_ref, pi_ref, pw_ref, *rest):
@@ -298,7 +298,7 @@
             pltpu.VMEM((2, 256, 128 * n), BF16),
             pltpu.VMEM((768, 384), BF16),
             pltpu.VMEM((768, 384), BF16),
-            pltpu.VMEM((8, 288, 256 * n), BF16),
+            pltpu.VMEM((8, 192, 256 * n), BF16),
             pltpu.VMEM((2 * n, NT2, 128), F32),
         ],
         compiler_params=ROOMY,
@@ -312,7 +312,7 @@
         operators_kernel,
         in_specs=[SMEM, VMEM],
         out_specs=[VMEM, VMEM],
-        out_shape=[jax.ShapeDtypeStruct((NDISP * SLOT, 128), F32)] * 2,
+        out_shape=[jax.ShapeDtypeStruct((NDISP * slot, 128), F32) for slot in (SLOT, SLOT // 2)],
         compiler_params=ROOMY,
         cost_estimate=cost(10**6, 10**7),
         name="operators",
@@ -379,7 +379,8 @@
     holder, p = src // 4, src % 4
     far = jnp.where((holder // 32) % 2 == core, 0, 1)
     src_at = ((far * CHIPS + (holder // 64) * 32 + holder % 32) * PARENTS + p) * SLOT
-    disp_at = mine(partner_disp) * SLOT
+    disp1 = mine(partner_disp) * SLOT
+    disp2 = disp1 // 2
     ops, = together(translation.transpose(0, 2, 1, 3).reshape(NDISP * 6, 2, NP2))
     ops = ops.reshape(NDISP * 6, 2, 3, 128).transpose(0, 2, 1, 3).reshape(NDISP * 36, 128)
 
@@ -388,16 +389,16 @@
     x2, _ = together(x, out1)
     out2, cosine, sine = aggregate(SECOND, True)(child_octant, x2, shift_angle, *stencils)
     ops1, ops2 = operators()(zh.reshape(1), ops)
-    got1, out2, ops1, ops2, src_at, disp_at = together(got1, out2, ops1, ops2, src_at, disp_at)
+    got1, out2, ops1, ops2, src_at, disp1, disp2 = together(got1, out2, ops1, ops2, src_at, disp1, disp2)
 
     got2 = exchange(out2)
     other1 = lax.ppermute(got1, "c", swap)
-    in1 = translate(FIRST)(src_at, disp_at, got1, other1, ops1)
+    in1 = translate(FIRST)(src_at, disp1, got1, other1, ops1)
     in1, got2 = together(in1, got2)
 
     back1 = exchange(in1)
     other2 = lax.ppermute(got2, "c", swap)
-    in2 = translate(SECOND)(src_at, disp_at, got2, other2, ops2)
+    in2 = translate(SECOND)(src_at, disp2, got2, other2, ops2)
     in2, back1 = together(in2, back1)
 
     back2 = exchange(in2)

time: 133 us -> 133 us (level)
  Pallas kernels: 79.3 us -> 77.5 us
  waiting for transfers between devices: 20.7 us -> 22.2 us
    all_to_all x4, waiting for transfers between devices: 18.5 us -> 19.9 us  [exchange(): lax.all_to_all(a.reshape(CHIPS, -1, 128), CHIP, 0, 0, tiled=True)]
  transfers between devices with their start and end apart: 6 -> 6, of which waited for: 5 -> 5; matrix products, arithmetic and copies ran while one was open for 0% -> 0% of each run, Pallas kernels for 44% -> 43%
where the time goes in v6:
time: 133 us; the launch traced here: 132 us
  Pallas kernels  77.5 us (58%)
  starting transfers between devices  30.8 us (23%)
  waiting for transfers between devices  22.2 us (17%)
    all_to_all x4, starting transfers between devices, exchange(): lax.all_to_all(a.reshape(CHIPS, -1, 128), CHIP, 0, 0, tiled=True)  30.8 us
    all_to_all x4, waiting for transfers between devices, exchange(): lax.all_to_all(a.reshape(CHIPS, -1, 128), CHIP, 0, 0, tiled=True)  19.9 us
    pallas_call x1, Pallas kernels, local(): in1 = translate(FIRST)(src_at, disp1, got1, other1, ops1)  14.8 us
    pallas_call x1, Pallas kernels, local(): in2 = translate(SECOND)(src_at, disp2, got2, other2, ops2)  13.7 us
    pallas_call x1, Pallas kernels, local(): out1, = aggregate(FIRST, False)(child_octant, x, shift_angle, *stencils)  12.4 us
    pallas_call x1, Pallas kernels, local(): aggregate(SECOND, True)(child_octant, x2, shift_angle, *stencils)  11.8 us
    pallas_call x1, Pallas kernels, local(): y = disaggregate(FIRST, 0)(child_octant, back1, cosine, sine, *stencils)  11 us
    pallas_call x1, Pallas kernels, local(): y = disaggregate(SECOND, 1)(child_octant, back2, cosine, sine, *stencils, y)  8.03 us
  transfers between devices with their start and end apart: 6, of which 5 were waited for; matrix products, arithmetic and copies ran while one was open for 0% of the time, Pallas kernels for 43%

profile of v6, /device:TPU:0, one launch (start us, length us, event | category | flops | bytes accessed | tf_op | source)
XLA Modules:
  0.0 131.9 jit_solution(16558829294946372502)
XLA Ops:
  0.0 12.4 %aggregate2.1 = f32[3072,128]{1,0:T(8,128)} custom-call(s32[4,8]{1,0:T(4,128)} %oct_ref.7, f32[9216,128]{1,0:T(8,128)} %bitcast.63, f32[8,192,384]{2,1,0:T(8,128)} %angle_ref.3, s32[4,192]{1,0:T(4,128)} %bitcast.49, f32[4,192]{1,0:T(4,128)} %bitcast.53, s32[4,384]{1,0:T(4,128)} %bitcast.41, f32[4,384]{1,0:T(4,128)} %bitcast.45), custom_call_target="tpu_custom_call" | custom-call | flops 8000000000 | bytes 10000000 | tf_op jit(solution)/shard_map/aggregate2/pallas_call | solution.py:387
  12.4 11.9 %all-to-all-start = ((f32[64,48,128]{2,1,0:T(8,128)}), f32[64,48,128]{2,1,0:T(8,128)}, u32[]{:S(2)}, u32[]{:S(2)}) async-start(f32[64,48,128]{2,1,0:T(8,128)} %bitcast.58), calls=%async_computation | async-start | bytes 3145728 | tf_op jit(solution)/shard_map/all_to_all | solution.py:358
  24.4 5.8 %operators.1 = (f32[5056,128]{1,0:T(8,128)}, f32[2528,128]{1,0:T(8,128)}) custom-call(s32[1]{0:T(128)} %bitcast.11.zh_ref, f32[11376,128]{1,0:T(8,128)} %bitcast.57), custom_call_target="tpu_custom_call" | custom-call | flops 1000000 | bytes 10000000 | tf_op jit(solution)/shard_map/operators/pallas_call | solution.py:391
  30.3 0.1 add_select_fusion
  30.4 11.8 %aggregate1.1 = (f32[1536,128]{1,0:T(8,128)}, f32[8,192,384]{2,1,0:T(8,128)}, f32[8,192,384]{2,1,0:T(8,128)}) custom-call(s32[4,8]{1,0:T(4,128)} %oct_ref.7, f32[9216,128]{1,0:T(8,128)} %bitcast.64, f32[8,192,384]{2,1,0:T(8,128)} %angle_ref.3, s32[4,192]{1,0:T(4,128)} %bitcast.50, f32[4,192]{1,0:T(4,128)} %bitcast.54, s32[4,384]{1,0:T(4,128)} %bitcast.42, ...), custom_call_target="tpu_custom_call" | custom-call | flops 4000000000 | bytes 10000000 | tf_op jit(solution)/shard_map/aggregate1/pallas_call | solution.py:390
  42.2 6.4 %all-to-all-done = f32[64,48,128]{2,1,0:T(8,128)} async-done(((f32[64,48,128]{2,1,0:T(8,128)}), f32[64,48,128]{2,1,0:T(8,128)}, u32[]{:S(2)}, u32[]{:S(2)}) %all-to-all-start) | async-done | bytes 1572896 | tf_op jit(solution)/shard_map/all_to_all | solution.py:358
  48.6 5.1 %all-to-all-start.1 = ((f32[64,24,128]{2,1,0:T(8,128)}), f32[64,24,128]{2,1,0:T(8,128)S(1)}, u32[]{:S(2)}, u32[]{:S(2)}) async-start(f32[64,24,128]{2,1,0:T(8,128)} %bitcast.59), calls=%async_computation.1 | async-start | bytes 1572864 | tf_op jit(solution)/shard_map/all_to_all | solution.py:358
  53.7 14.8 %translate2.1 = f32[3072,128]{1,0:T(8,128)} custom-call(s32[8192]{0:T(1024)S(1)} %get-tuple-element.28.src_ref, s32[8192]{0:T(1024)S(1)} %bitcast.40, f32[3072,128]{1,0:T(8,128)} %bitcast.8.own_ref, f32[3072,128]{1,0:T(8,128)} %collective-permute-done.other_ref, f32[5056,128]{1,0:T(8,128)} %get-tuple-element.32.t_ref), custom_call_target="tpu_custom_call" | custom-call | flops 100000000 | bytes 10000000 | tf_op jit(solution)/shard_map/translate2/pallas_call | solution.py:396
  68.5 2.0 %all-to-all-done.1 = f32[64,24,128]{2,1,0:T(8,128)S(1)} async-done(((f32[64,24,128]{2,1,0:T(8,128)}), f32[64,24,128]{2,1,0:T(8,128)S(1)}, u32[]{:S(2)}, u32[]{:S(2)}) %all-to-all-start.1) | async-done | bytes 786464 | tf_op jit(solution)/shard_map/all_to_all | solution.py:358
  70.5 8.3 %all-to-all-start.2 = ((f32[64,48,128]{2,1,0:T(8,128)}), f32[64,48,128]{2,1,0:T(8,128)S(1)}, u32[]{:S(2)}, u32[]{:S(2)}) async-start(f32[64,48,128]{2,1,0:T(8,128)} %bitcast.23), calls=%async_computation.2 | async-start | bytes 3145728 | tf_op jit(solution)/shard_map/all_to_all | solution.py:358
  78.9 0.0 copy-start
  78.9 0.0 copy-start.1
  78.9 0.0 copy-start.2
  78.9 0.0 copy-start.3
  78.9 0.0 copy-start.4
  78.9 0.1 collective-permute-start.1
  79.0 2.3 %collective-permute-done.1.other_ref = f32[1536,128]{1,0:T(8,128)S(1)} collective-permute-done((f32[1536,128]{1,0:T(8,128)S(1)}, f32[1536,128]{1,0:T(8,128)S(1)}, u32[]{:S(2)}, u32[]{:S(2)}) %collective-permute-start.1) | collective-permute-done | bytes 786464 | tf_op jit(solution)/shard_map/ppermute | solution.py:400
  81.3 0.9 copy-done.5
  82.2 13.7 %translate1.1 = f32[1536,128]{1,0:T(8,128)} custom-call(s32[8192]{0:T(1024)S(1)} %get-tuple-element.28.src_ref, s32[8192]{0:T(1024)S(1)} %get-tuple-element.29.disp_ref, f32[1536,128]{1,0:T(8,128)S(1)} %bitcast.36, f32[1536,128]{1,0:T(8,128)} %copy-done.5, f32[2528,128]{1,0:T(8,128)} %get-tuple-element.35.t_ref), custom_call_target="tpu_custom_call" | custom-call | flops 100000000 | bytes 10000000 | tf_op jit(solution)/shard_map/translate1/pallas_call | solution.py:401
  95.8 7.6 %all-to-all-done.2 = f32[64,48,128]{2,1,0:T(8,128)S(1)} async-done(((f32[64,48,128]{2,1,0:T(8,128)}), f32[64,48,128]{2,1,0:T(8,128)S(1)}, u32[]{:S(2)}, u32[]{:S(2)}) %all-to-all-start.2) | async-done | bytes 1572896 | tf_op jit(solution)/shard_map/all_to_all | solution.py:358
  103.4 5.4 %all-to-all-start.3 = ((f32[64,24,128]{2,1,0:T(8,128)}), f32[64,24,128]{2,1,0:T(8,128)S(1)}, u32[]{:S(2)}, u32[]{:S(2)}) async-start(f32[64,24,128]{2,1,0:T(8,128)} %bitcast.25), calls=%async_computation.3 | async-start | bytes 1572864 | tf_op jit(solution)/shard_map/all_to_all | solution.py:358
  108.8 11.0 %disaggregate2.1.rest_0_ = f32[9216,128]{1,0:T(8,128)} custom-call(s32[4,8]{1,0:T(4,128)S(1)} %copy-done.4, f32[3072,128]{1,0:T(8,128)S(1)} %bitcast.38, f32[8,192,384]{2,1,0:T(8,128)} %get-tuple-element.38.cos_ref, f32[8,192,384]{2,1,0:T(8,128)} %get-tuple-element.39.sin_ref, s32[4,192]{1,0:T(4,128)S(1)} %bitcast.51, f32[4,192]{1,0:T(4,128)S(1)} %bitcast.55, ...), custom_call_target="tpu_custom_call" | custom-call | flops 8000000000 | bytes 10000000 | tf_op jit(solution)/shard_map/disaggregate2/pallas_call | solution.py:405
  119.9 4.0 %all-to-all-done.3 = f32[64,24,128]{2,1,0:T(8,128)S(1)} async-done(((f32[64,24,128]{2,1,0:T(8,128)}), f32[64,24,128]{2,1,0:T(8,128)S(1)}, u32[]{:S(2)}, u32[]{:S(2)}) %all-to-all-start.3) | async-done | bytes 786464 | tf_op jit(solution)/shard_map/all_to_all | solution.py:358
  123.8 8.0 %disaggregate1.1 = f32[9216,128]{1,0:T(8,128)} custom-call(s32[4,8]{1,0:T(4,128)S(1)} %copy-done.4, f32[1536,128]{1,0:T(8,128)S(1)} %bitcast.37, f32[8,192,384]{2,1,0:T(8,128)} %get-tuple-element.38.cos_ref, f32[8,192,384]{2,1,0:T(8,128)} %get-tuple-element.39.sin_ref, s32[4,192]{1,0:T(4,128)S(1)} %bitcast.52, f32[4,192]{1,0:T(4,128)S(1)} %bitcast.56, ...), custom_call_target="tpu_custom_call" | custom-call | flops 4000000000 | bytes 10000000 | tf_op jit(solution)/shard_map/disaggregate1/pallas_call | solution.py:407
  (16 shorter events, 0.2 us)
Async XLA Ops:
  12.4 11.9 %copy-start.6 = (s32[512,32]{0,1:T(8,128)S(1)}, s32[512,32]{0,1:T(8,128)}, u32[]{:S(2)}) copy-start(s32[512,32]{0,1:T(8,128)} %param.17) | copy-start | bytes 196612
  12.4 12.0 %copy-start.7 = (s32[512,32]{0,1:T(8,128)S(1)}, s32[512,32]{0,1:T(8,128)}, u32[]{:S(2)}) copy-start(s32[512,32]{0,1:T(8,128)} %param.18) | copy-start | bytes 196612
  12.4 36.2 %all-to-all-start = ((f32[64,48,128]{2,1,0:T(8,128)}), f32[64,48,128]{2,1,0:T(8,128)}, u32[]{:S(2)}, u32[]{:S(2)}) async-start(f32[64,48,128]{2,1,0:T(8,128)} %bitcast.58), calls=%async_computation | async-start | bytes 3145728 | tf_op jit(solution)/shard_map/all_to_all | solution.py:358
  48.6 5.2 %collective-permute-start = (f32[3072,128]{1,0:T(8,128)}, f32[3072,128]{1,0:T(8,128)}, u32[]{:S(2)}, u32[]{:S(2)}) collective-permute-start(f32[3072,128]{1,0:T(8,128)} %bitcast.8.own_ref), channel_id=1, source_target_pairs={{0,32},{32,0},{1,33},{33,1},{2,34},{34,2},{3,35},{35,3},{4,36},{36... | collective-permute-start | bytes 4718600 | tf_op jit(solution)/shard_map/ppermute | solution.py:395
  48.6 21.9 %all-to-all-start.1 = ((f32[64,24,128]{2,1,0:T(8,128)}), f32[64,24,128]{2,1,0:T(8,128)S(1)}, u32[]{:S(2)}, u32[]{:S(2)}) async-start(f32[64,24,128]{2,1,0:T(8,128)} %bitcast.59), calls=%async_computation.1 | async-start | bytes 1572864 | tf_op jit(solution)/shard_map/all_to_all | solution.py:358
  70.5 32.9 %all-to-all-start.2 = ((f32[64,48,128]{2,1,0:T(8,128)}), f32[64,48,128]{2,1,0:T(8,128)S(1)}, u32[]{:S(2)}, u32[]{:S(2)}) async-start(f32[64,48,128]{2,1,0:T(8,128)} %bitcast.23), calls=%async_computation.2 | async-start | bytes 3145728 | tf_op jit(solution)/shard_map/all_to_all | solution.py:358
  78.9 29.9 %copy-start = (s32[384,4]{0,1:T(4,128)S(1)}, s32[384,4]{0,1:T(4,128)}, u32[]{:S(2)}) copy-start(s32[384,4]{0,1:T(4,128)} %param.14) | copy-start | bytes 18436
  78.9 29.9 %copy-start.1 = (f32[384,4]{0,1:T(4,128)S(1)}, f32[384,4]{0,1:T(4,128)}, u32[]{:S(2)}) copy-start(f32[384,4]{0,1:T(4,128)} %param.15) | copy-start | bytes 18436
  78.9 29.9 %copy-start.2 = (s32[192,4]{0,1:T(4,128)S(1)}, s32[192,4]{0,1:T(4,128)}, u32[]{:S(2)}) copy-start(s32[192,4]{0,1:T(4,128)} %param.12) | copy-start | bytes 9220
  78.9 29.9 %copy-start.3 = (f32[192,4]{0,1:T(4,128)S(1)}, f32[192,4]{0,1:T(4,128)}, u32[]{:S(2)}) copy-start(f32[192,4]{0,1:T(4,128)} %param.13) | copy-start | bytes 9220
  78.9 29.9 %copy-start.4 = (s32[4,8]{1,0:T(4,128)S(1)}, s32[4,8]{1,0:T(4,128)}, u32[]{:S(2)}) copy-start(s32[4,8]{1,0:T(4,128)} %oct_ref.7) | copy-start | bytes 388
  78.9 2.4 %collective-permute-start.1 = (f32[1536,128]{1,0:T(8,128)S(1)}, f32[1536,128]{1,0:T(8,128)S(1)}, u32[]{:S(2)}, u32[]{:S(2)}) collective-permute-start(f32[1536,128]{1,0:T(8,128)S(1)} %bitcast.35), channel_id=1, source_target_pairs={{0,32},{32,0},{1,33},{33,1},{2,34},{34,2},{3,35},{35,3},{4,36},{36... | collective-permute-start | bytes 2359304 | tf_op jit(solution)/shard_map/ppermute | solution.py:400
  81.3 0.9 copy-start.5
  103.4 20.4 %all-to-all-start.3 = ((f32[64,24,128]{2,1,0:T(8,128)}), f32[64,24,128]{2,1,0:T(8,128)S(1)}, u32[]{:S(2)}, u32[]{:S(2)}) async-start(f32[64,24,128]{2,1,0:T(8,128)} %bitcast.25), calls=%async_computation.3 | async-start | bytes 1572864 | tf_op jit(solution)/shard_map/all_to_all | solution.py:358

commit v7 on v6

--- a/solution.py
+++ b/solution.py
@@ -259,7 +259,7 @@
 VMEM = pl.BlockSpec(memory_space=pltpu.VMEM)
 SMEM = pl.BlockSpec(memory_space=pltpu.SMEM)
 STENCILS = [whole((4, NT2)), whole((4, NT2)), whole((4, NP2)), whole((4, NP2))]
-PARAMS = pltpu.CompilerParams(vmem_limit_bytes=52 * 2**20)
+PARAMS = pltpu.CompilerParams(vmem_limit_bytes=50 * 2**20)
 ROOMY = pltpu.CompilerParams(vmem_limit_bytes=60 * 2**20)
 CHILDREN = pl.BlockSpec((8 * 288, 128), lambda p: (p, 0))
 

time: 133 us -> 133 us (level)
  local copies, waits for them, and re-layouts: 1.04 us -> 5.67 us
  waiting for transfers between devices: 22.2 us -> 19.6 us
    unnamed x16 -> x24, local copies, waits for them, and re-layouts: 0.92 us -> 5.55 us
    all_to_all x4, waiting for transfers between devices: 19.9 us -> 17.3 us  [exchange(): lax.all_to_all(a.reshape(CHIPS, -1, 128), CHIP, 0, 0, tiled=True)]
where the time goes in v7:
time: 133 us; the launch traced here: 132 us
  Pallas kernels  76.5 us (58%)
  starting transfers between devices  30.3 us (23%)
  waiting for transfers between devices  19.6 us (15%)
  local copies, waits for them, and re-layouts  5.67 us (4%)
    all_to_all x4, starting transfers between devices, exchange(): lax.all_to_all(a.reshape(CHIPS, -1, 128), CHIP, 0, 0, tiled=True)  30.2 us
    all_to_all x4, waiting for transfers between devices, exchange(): lax.all_to_all(a.reshape(CHIPS, -1, 128), CHIP, 0, 0, tiled=True)  17.3 us
    pallas_call x1, Pallas kernels, local(): in1 = translate(FIRST)(src_at, disp1, got1, other1, ops1)  14.3 us
    pallas_call x1, Pallas kernels, local(): in2 = translate(SECOND)(src_at, disp2, got2, other2, ops2)  13.7 us
    pallas_call x1, Pallas kernels, local(): out1, = aggregate(FIRST, False)(child_octant, x, shift_angle, *stencils)  12.4 us
    pallas_call x1, Pallas kernels, local(): aggregate(SECOND, True)(child_octant, x2, shift_angle, *stencils)  11.8 us
    pallas_call x1, Pallas kernels, local(): y = disaggregate(FIRST, 0)(child_octant, back1, cosine, sine, *stencils)  10.8 us
    pallas_call x1, Pallas kernels, local(): y = disaggregate(SECOND, 1)(child_octant, back2, cosine, sine, *stencils, y)  7.79 us
  transfers between devices with their start and end apart: 6, of which 5 were waited for; matrix products, arithmetic and copies ran while one was open for 0% of the time, Pallas kernels for 43%

profile of v7, /device:TPU:0, one launch (start us, length us, event | category | flops | bytes accessed | tf_op | source)
XLA Modules:
  0.0 132.4 jit_solution(3934244350642370882)
XLA Ops:
  0.0 12.4 %aggregate2.1 = f32[3072,128]{1,0:T(8,128)} custom-call(s32[4,8]{1,0:T(4,128)} %oct_ref.7, f32[9216,128]{1,0:T(8,128)} %bitcast.65, f32[8,192,384]{2,1,0:T(8,128)} %angle_ref.3, s32[4,192]{1,0:T(4,128)} %bitcast.51, f32[4,192]{1,0:T(4,128)} %bitcast.55, s32[4,384]{1,0:T(4,128)} %bitcast.43, f32[4,384]{1,0:T(4,128)} %bitcast.47), custom_call_target="tpu_custom_call" | custom-call | flops 8000000000 | bytes 10000000 | tf_op jit(solution)/shard_map/aggregate2/pallas_call | solution.py:387
  12.4 11.6 %all-to-all-start = ((f32[64,48,128]{2,1,0:T(8,128)}), f32[64,48,128]{2,1,0:T(8,128)S(1)}, u32[]{:S(2)}, u32[]{:S(2)}) async-start(f32[64,48,128]{2,1,0:T(8,128)} %bitcast.60), calls=%async_computation | async-start | bytes 3145728 | tf_op jit(solution)/shard_map/all_to_all | solution.py:358
  24.2 5.8 %operators.1 = (f32[5056,128]{1,0:T(8,128)}, f32[2528,128]{1,0:T(8,128)}) custom-call(s32[1]{0:T(128)} %bitcast.11.zh_ref, f32[11376,128]{1,0:T(8,128)} %bitcast.59), custom_call_target="tpu_custom_call" | custom-call | flops 1000000 | bytes 10000000 | tf_op jit(solution)/shard_map/operators/pallas_call | solution.py:391
  30.0 0.1 add_select_fusion
  30.2 11.8 %aggregate1.1 = (f32[1536,128]{1,0:T(8,128)}, f32[8,192,384]{2,1,0:T(8,128)}, f32[8,192,384]{2,1,0:T(8,128)}) custom-call(s32[4,8]{1,0:T(4,128)} %oct_ref.7, f32[9216,128]{1,0:T(8,128)} %bitcast.66, f32[8,192,384]{2,1,0:T(8,128)} %angle_ref.3, s32[4,192]{1,0:T(4,128)} %bitcast.52, f32[4,192]{1,0:T(4,128)} %bitcast.56, s32[4,384]{1,0:T(4,128)} %bitcast.44, ...), custom_call_target="tpu_custom_call" | custom-call | flops 4000000000 | bytes 10000000 | tf_op jit(solution)/shard_map/aggregate1/pallas_call | solution.py:390
  41.9 6.5 %all-to-all-done = f32[64,48,128]{2,1,0:T(8,128)S(1)} async-done(((f32[64,48,128]{2,1,0:T(8,128)}), f32[64,48,128]{2,1,0:T(8,128)S(1)}, u32[]{:S(2)}, u32[]{:S(2)}) %all-to-all-start) | async-done | bytes 1572896 | tf_op jit(solution)/shard_map/all_to_all | solution.py:358
  48.5 0.0 collective-permute-start
  48.5 5.1 %all-to-all-start.1 = ((f32[64,24,128]{2,1,0:T(8,128)}), f32[64,24,128]{2,1,0:T(8,128)S(1)}, u32[]{:S(2)}, u32[]{:S(2)}) async-start(f32[64,24,128]{2,1,0:T(8,128)} %bitcast.61), calls=%async_computation.1 | async-start | bytes 1572864 | tf_op jit(solution)/shard_map/all_to_all | solution.py:358
  53.6 14.3 %translate2.1 = f32[3072,128]{1,0:T(8,128)} custom-call(s32[8192]{0:T(1024)S(1)} %get-tuple-element.28.src_ref, s32[8192]{0:T(1024)S(1)} %bitcast.42, f32[3072,128]{1,0:T(8,128)S(1)} %bitcast.36, f32[3072,128]{1,0:T(8,128)} %collective-permute-done.other_ref, f32[5056,128]{1,0:T(8,128)} %get-tuple-element.32.t_ref), custom_call_target="tpu_custom_call" | custom-call | flops 100000000 | bytes 10000000 | tf_op jit(solution)/shard_map/translate2/pallas_call | solution.py:396
  68.0 2.5 %all-to-all-done.1 = f32[64,24,128]{2,1,0:T(8,128)S(1)} async-done(((f32[64,24,128]{2,1,0:T(8,128)}), f32[64,24,128]{2,1,0:T(8,128)S(1)}, u32[]{:S(2)}, u32[]{:S(2)}) %all-to-all-start.1) | async-done | bytes 786464 | tf_op jit(solution)/shard_map/all_to_all | solution.py:358
  70.4 0.0 copy-start.9
  70.4 8.0 %all-to-all-start.2 = ((f32[64,48,128]{2,1,0:T(8,128)}), f32[64,48,128]{2,1,0:T(8,128)S(1)}, u32[]{:S(2)}, u32[]{:S(2)}) async-start(f32[64,48,128]{2,1,0:T(8,128)} %bitcast.23), calls=%async_computation.2 | async-start | bytes 3145728 | tf_op jit(solution)/shard_map/all_to_all | solution.py:358
  78.5 0.1 collective-permute-start.1
  78.6 2.3 %collective-permute-done.1.other_ref = f32[1536,128]{1,0:T(8,128)S(1)} collective-permute-done((f32[1536,128]{1,0:T(8,128)S(1)}, f32[1536,128]{1,0:T(8,128)S(1)}, u32[]{:S(2)}, u32[]{:S(2)}) %collective-permute-start.1) | collective-permute-done | bytes 786464 | tf_op jit(solution)/shard_map/ppermute | solution.py:400
  80.9 1.3 copy-done.4
  82.2 13.7 %translate1.1 = f32[1536,128]{1,0:T(8,128)} custom-call(s32[8192]{0:T(1024)S(1)} %get-tuple-element.28.src_ref, s32[8192]{0:T(1024)S(1)} %get-tuple-element.29.disp_ref, f32[1536,128]{1,0:T(8,128)S(1)} %bitcast.38, f32[1536,128]{1,0:T(8,128)S(1)} %collective-permute-done.1.other_ref, f32[2528,128]{1,0:T(8,128)S(1)} %copy-done.4), custom_call_target="tpu_custom_call" | custom-call | flops 100000000 | bytes 10000000 | tf_op jit(solution)/shard_map/translate1/pallas_call | solution.py:401
  95.8 7.2 %all-to-all-done.2 = f32[64,48,128]{2,1,0:T(8,128)S(1)} async-done(((f32[64,48,128]{2,1,0:T(8,128)}), f32[64,48,128]{2,1,0:T(8,128)S(1)}, u32[]{:S(2)}, u32[]{:S(2)}) %all-to-all-start.2) | async-done | bytes 1572896 | tf_op jit(solution)/shard_map/all_to_all | solution.py:358
  103.0 1.1 copy-done.2
  104.2 5.4 %all-to-all-start.3 = ((f32[64,24,128]{2,1,0:T(8,128)}), f32[64,24,128]{2,1,0:T(8,128)S(1)}, u32[]{:S(2)}, u32[]{:S(2)}) async-start(f32[64,24,128]{2,1,0:T(8,128)} %bitcast.25), calls=%async_computation.3 | async-start | bytes 1572864 | tf_op jit(solution)/shard_map/all_to_all | solution.py:358
  109.6 1.7 %copy-done = f32[8,192,384]{2,1,0:T(8,128)S(1)} copy-done((f32[8,192,384]{2,1,0:T(8,128)S(1)}, f32[8,192,384]{2,1,0:T(8,128)}, u32[]{:S(2)}) %copy-start) | copy-done | bytes 2359320
  111.3 1.4 %copy-done.3 = f32[64,48,128]{2,1,0:T(8,128)S(1)} copy-done((f32[64,48,128]{2,1,0:T(8,128)S(1)}, f32[64,48,128]{2,1,0:T(8,128)}, u32[]{:S(2)}) %copy-start.3) | copy-done | bytes 1572888
  112.7 10.8 %disaggregate2.1.rest_0_ = f32[9216,128]{1,0:T(8,128)} custom-call(s32[4,8]{1,0:T(4,128)S(1)} %copy-done.9, f32[3072,128]{1,0:T(8,128)S(1)} %bitcast.40, f32[8,192,384]{2,1,0:T(8,128)S(1)} %copy-done, f32[8,192,384]{2,1,0:T(8,128)} %get-tuple-element.39.sin_ref, s32[4,192]{1,0:T(4,128)S(1)} %bitcast.53, f32[4,192]{1,0:T(4,128)S(1)} %bitcast.57, ...), custom_call_target="tpu_custom_call" | custom-call | flops 8000000000 | bytes 10000000 | tf_op jit(solution)/shard_map/disaggregate2/pallas_call | solution.py:405
  123.5 1.1 all-to-all-done.3
  124.6 7.8 %disaggregate1.1 = f32[9216,128]{1,0:T(8,128)} custom-call(s32[4,8]{1,0:T(4,128)S(1)} %copy-done.9, f32[1536,128]{1,0:T(8,128)S(1)} %bitcast.39, f32[8,192,384]{2,1,0:T(8,128)S(1)} %copy-done.1, f32[8,192,384]{2,1,0:T(8,128)} %get-tuple-element.39.sin_ref, s32[4,192]{1,0:T(4,128)S(1)} %bitcast.54, f32[4,192]{1,0:T(4,128)S(1)} %bitcast.58, ...), custom_call_target="tpu_custom_call" | custom-call | flops 4000000000 | bytes 10000000 | tf_op jit(solution)/shard_map/disaggregate1/pallas_call | solution.py:407
  (24 shorter events, 0.2 us)
Async XLA Ops:
  12.4 11.7 %copy-start.10 = (s32[512,32]{0,1:T(8,128)S(1)}, s32[512,32]{0,1:T(8,128)}, u32[]{:S(2)}) copy-start(s32[512,32]{0,1:T(8,128)} %param.17) | copy-start | bytes 196612
  12.4 11.7 %copy-start.11 = (s32[512,32]{0,1:T(8,128)S(1)}, s32[512,32]{0,1:T(8,128)}, u32[]{:S(2)}) copy-start(s32[512,32]{0,1:T(8,128)} %param.18) | copy-start | bytes 196612
  12.4 36.1 %all-to-all-start = ((f32[64,48,128]{2,1,0:T(8,128)}), f32[64,48,128]{2,1,0:T(8,128)S(1)}, u32[]{:S(2)}, u32[]{:S(2)}) async-start(f32[64,48,128]{2,1,0:T(8,128)} %bitcast.60), calls=%async_computation | async-start | bytes 3145728 | tf_op jit(solution)/shard_map/all_to_all | solution.py:358
  48.5 5.2 %collective-permute-start = (f32[3072,128]{1,0:T(8,128)S(1)}, f32[3072,128]{1,0:T(8,128)}, u32[]{:S(2)}, u32[]{:S(2)}) collective-permute-start(f32[3072,128]{1,0:T(8,128)S(1)} %bitcast.35), channel_id=1, source_target_pairs={{0,32},{32,0},{1,33},{33,1},{2,34},{34,2},{3,35},{35,3},{4,36},{36... | collective-permute-start | bytes 4718600 | tf_op jit(solution)/shard_map/ppermute | solution.py:395
  48.5 21.9 %all-to-all-start.1 = ((f32[64,24,128]{2,1,0:T(8,128)}), f32[64,24,128]{2,1,0:T(8,128)S(1)}, u32[]{:S(2)}, u32[]{:S(2)}) async-start(f32[64,24,128]{2,1,0:T(8,128)} %bitcast.61), calls=%async_computation.1 | async-start | bytes 1572864 | tf_op jit(solution)/shard_map/all_to_all | solution.py:358
  70.4 39.2 %copy-start.5 = (s32[384,4]{0,1:T(4,128)S(1)}, s32[384,4]{0,1:T(4,128)}, u32[]{:S(2)}) copy-start(s32[384,4]{0,1:T(4,128)} %param.14) | copy-start | bytes 18436
  70.4 39.2 %copy-start.6 = (f32[384,4]{0,1:T(4,128)S(1)}, f32[384,4]{0,1:T(4,128)}, u32[]{:S(2)}) copy-start(f32[384,4]{0,1:T(4,128)} %param.15) | copy-start | bytes 18436
  70.4 39.2 %copy-start.7 = (s32[192,4]{0,1:T(4,128)S(1)}, s32[192,4]{0,1:T(4,128)}, u32[]{:S(2)}) copy-start(s32[192,4]{0,1:T(4,128)} %param.12) | copy-start | bytes 9220
  70.4 39.2 %copy-start.8 = (f32[192,4]{0,1:T(4,128)S(1)}, f32[192,4]{0,1:T(4,128)}, u32[]{:S(2)}) copy-start(f32[192,4]{0,1:T(4,128)} %param.13) | copy-start | bytes 9220
  70.4 39.2 %copy-start.9 = (s32[4,8]{1,0:T(4,128)S(1)}, s32[4,8]{1,0:T(4,128)}, u32[]{:S(2)}) copy-start(s32[4,8]{1,0:T(4,128)} %oct_ref.7) | copy-start | bytes 388
  70.4 32.6 %all-to-all-start.2 = ((f32[64,48,128]{2,1,0:T(8,128)}), f32[64,48,128]{2,1,0:T(8,128)S(1)}, u32[]{:S(2)}, u32[]{:S(2)}) async-start(f32[64,48,128]{2,1,0:T(8,128)} %bitcast.23), calls=%async_computation.2 | async-start | bytes 3145728 | tf_op jit(solution)/shard_map/all_to_all | solution.py:358
  78.5 2.4 %collective-permute-start.1 = (f32[1536,128]{1,0:T(8,128)S(1)}, f32[1536,128]{1,0:T(8,128)S(1)}, u32[]{:S(2)}, u32[]{:S(2)}) collective-permute-start(f32[1536,128]{1,0:T(8,128)S(1)} %bitcast.37), channel_id=1, source_target_pairs={{0,32},{32,0},{1,33},{33,1},{2,34},{34,2},{3,35},{35,3},{4,36},{36... | collective-permute-start | bytes 2359304 | tf_op jit(solution)/shard_map/ppermute | solution.py:400
  80.9 1.3 copy-start.4
  103.0 1.1 copy-start.2
  104.2 20.4 %all-to-all-start.3 = ((f32[64,24,128]{2,1,0:T(8,128)}), f32[64,24,128]{2,1,0:T(8,128)S(1)}, u32[]{:S(2)}, u32[]{:S(2)}) async-start(f32[64,24,128]{2,1,0:T(8,128)} %bitcast.25), calls=%async_computation.3 | async-start | bytes 1572864 | tf_op jit(solution)/shard_map/all_to_all | solution.py:358
  109.6 1.7 %copy-start = (f32[8,192,384]{2,1,0:T(8,128)S(1)}, f32[8,192,384]{2,1,0:T(8,128)}, u32[]{:S(2)}) copy-start(f32[8,192,384]{2,1,0:T(8,128)} %get-tuple-element.38.cos_ref) | copy-start | bytes 7077892
  111.3 1.4 %copy-start.3 = (f32[64,48,128]{2,1,0:T(8,128)S(1)}, f32[64,48,128]{2,1,0:T(8,128)}, u32[]{:S(2)}) copy-start(f32[64,48,128]{2,1,0:T(8,128)} %copy-done.2) | copy-start | bytes 4718596
  112.7 11.9 %copy-start.1 = (f32[8,192,384]{2,1,0:T(8,128)S(1)}, f32[8,192,384]{2,1,0:T(8,128)}, u32[]{:S(2)}) copy-start(f32[8,192,384]{2,1,0:T(8,128)} %get-tuple-element.38.cos_ref) | copy-start | bytes 7077892
